TPU v7x, 256 devices: a whole 4x4x8 slice. The times are simulated.
256 devices in a mesh: frame: 16 (over z_hi, x, core), within: 16 (over y, z_lo).
Axes of the slice: x: 4, y: 4, z: 8 (z_hi: 2, z_lo: 4; z = z_hi * 4 + z_lo), core: 2. Of those that a mesh axis runs over, the one named last changes fastest.
Arguments:
- queries: bfloat16 [16, 1152, 1024], P('frame', 'within'), may hold values from -6 to 6
- keys_in: bfloat16 [16, 1152, 1024], P('frame', 'within'), may hold values from -6 to 6
- values_in: bfloat16 [16, 1152, 1024], P('frame', 'within'), may hold values from -6 to 6
- grad_out: bfloat16 [16, 1152, 1024], P('frame', 'within'), may hold values from -6 to 6
- partners: int32 [16, 2], replicated, may hold values from 0 to 15
- registers: int32 [16], replicated, may hold values from 1 to 288
Outputs:
- grad_queries: bfloat16 [16, 1152, 1024], P('frame', 'within')
- grad_keys: bfloat16 [16, 1152, 1024], P('frame', 'within')
- grad_values: bfloat16 [16, 1152, 1024], P('frame', 'within')
Inputs may be any that keep to these rules, and one draw needn't show every extreme that they name: `partners`: A row may list a group more than once, and may list its own group.
All inputs are finite; a program needn't handle non-finite values.
Results may differ from a plain program's by a relative error of at most 0.012.
Values may be sent and summed in bfloat16 or wider, within the bound.
No kernel may reach another device: no remote copies, remote signals or barrier semaphores. Data moves between devices by JAX's collectives and lax.ppermute only.
A program may use at most 128 MiB of HBM per device.

v0:
```python
import jax
import jax.numpy as jnp
from jax import lax
from jax.sharding import PartitionSpec as P

DH = 64


def local(queries, keys_in, values_in, grad_out, partners, registers):
    q_wide, k_wide, v_wide, d_wide = (
        lax.all_to_all(queries, "within", split_axis=2, concat_axis=1, tiled=True),
        lax.all_to_all(keys_in, "within", split_axis=2, concat_axis=1, tiled=True),
        lax.all_to_all(values_in, "within", split_axis=2, concat_axis=1, tiled=True),
        lax.all_to_all(grad_out, "within", split_axis=2, concat_axis=1, tiled=True),
    )
    seq = q_wide.shape[1]
    cols = q_wide.shape[2]
    heads_here = cols // DH
    scale = DH ** (-0.5)

    def split_heads(block):
        return block.reshape(seq, heads_here, DH)

    query3 = split_heads(q_wide[0])
    key3 = split_heads(k_wide[0])
    value3 = split_heads(v_wide[0])
    cotan3 = split_heads(d_wide[0])
    group = lax.axis_index("frame")
    listed = partners[group]
    positions = jnp.arange(seq, dtype=jnp.int32)
    everyone = jnp.ones((seq,), jnp.float32)
    groups = lax.axis_size("frame") * queries.shape[0]

    def patches(other):
        return (positions >= registers[other]).astype(jnp.float32)

    def logits(keys_here, visible):
        raw = (
            jnp.einsum("qhd,khd->hqk", query3, keys_here, preferred_element_type=jnp.float32)
            * scale
        )
        return jnp.where(visible[None, None, :] > 0, raw, -1e30)

    def stats(state, keys_here, values_here, visible, weight):
        old_top, old_total, old_dsum = state
        raw = logits(keys_here, visible)
        top = jnp.max(raw, axis=2)
        expo = jnp.exp(raw - top[:, :, None])
        dprod = jnp.einsum("qhd,khd->hqk", cotan3, values_here, preferred_element_type=jnp.float32)
        total = weight * jnp.sum(expo, axis=2)
        dsum = weight * jnp.sum(expo * dprod, axis=2)
        new_top = jnp.maximum(old_top, top)
        keep_old = jnp.exp(old_top - new_top)
        keep_new = jnp.exp(top - new_top)
        return (
            new_top,
            old_total * keep_old + total * keep_new,
            old_dsum * keep_old + dsum * keep_new,
        )

    def grads(final, keys_here, values_here, visible, weight):
        top, total, delta = final
        raw = logits(keys_here, visible)
        prob = jnp.exp(raw - top[:, :, None]) / total[:, :, None]
        dprod = jnp.einsum("qhd,khd->hqk", cotan3, values_here, preferred_element_type=jnp.float32)
        dscore = prob * (dprod - delta[:, :, None])
        dscore_low = dscore.astype(jnp.bfloat16)
        dq_add = jnp.einsum(
            "hqk,khd->qhd", dscore_low, keys_here, preferred_element_type=jnp.float32
        ) * (scale * weight)
        prob_low = prob.astype(jnp.bfloat16)
        dk_add = jnp.einsum(
            "hqk,qhd->khd", dscore_low, query3, preferred_element_type=jnp.float32
        ) * (scale * weight)
        dv_add = (
            jnp.einsum("hqk,qhd->khd", prob_low, cotan3, preferred_element_type=jnp.float32)
            * weight
        )
        return (dq_add.reshape(seq, cols), dk_add.reshape(seq, cols), dv_add.reshape(seq, cols))

    blank = jnp.zeros((heads_here, seq), jnp.float32)
    state = stats((blank - 1e30, blank, blank), key3, value3, everyone, 1.0)
    keys_all, values_all = (
        lax.all_gather(k_wide, "frame", axis=0, tiled=True),
        lax.all_gather(v_wide, "frame", axis=0, tiled=True),
    )
    for slot in range(listed.shape[0]):
        other = listed[slot]
        state = stats(
            state, split_heads(keys_all[other]), split_heads(values_all[other]), patches(other), 1.0
        )
    top, total, dsum = state
    final = (top, total, dsum / total)
    own_terms = grads(final, key3, value3, everyone, 1.0)
    empty = jnp.zeros((groups, seq, cols), jnp.float32)
    results = (own_terms[0], empty.at[group].add(own_terms[1]), empty.at[group].add(own_terms[2]))
    for slot in range(listed.shape[0]):
        other = listed[slot]
        added = grads(
            final, split_heads(keys_all[other]), split_heads(values_all[other]), patches(other), 1.0
        )
        results = (
            results[0] + added[0],
            results[1].at[other].add(added[1]),
            results[2].at[other].add(added[2]),
        )
    dq_sum = results[0]
    dk_mine, dv_mine = (
        lax.psum_scatter(results[1], "frame", scatter_dimension=0, tiled=True),
        lax.psum_scatter(results[2], "frame", scatter_dimension=0, tiled=True),
    )
    dq_low = dq_sum.astype(jnp.bfloat16)[None]
    dk_low = dk_mine.astype(jnp.bfloat16)
    dv_low = dv_mine.astype(jnp.bfloat16)
    return (
        lax.all_to_all(dq_low, "within", split_axis=1, concat_axis=2, tiled=True),
        lax.all_to_all(dk_low, "within", split_axis=1, concat_axis=2, tiled=True),
        lax.all_to_all(dv_low, "within", split_axis=1, concat_axis=2, tiled=True),
    )


def solution(mesh):
    placed = (
        P("frame", "within", None),
        P("frame", "within", None),
        P("frame", "within", None),
        P("frame", "within", None),
        P(),
        P(),
    )
    return jax.shard_map(
        local,
        mesh=mesh,
        in_specs=placed,
        out_specs=(
            P("frame", "within", None),
            P("frame", "within", None),
            P("frame", "within", None),
        ),
        check_vma=False,
    )
```

profile of v0, /device:TPU:2, one launch (start us, length us, event | category | flops | bytes accessed | tf_op | source)
XLA Modules:
  0.0 439.3 jit_solution(8207483100817958708)
XLA Ops:
  11.8 17.1 %all_to_all.120 = bf16[16,2,2304]{2,1,0:T(2,128)(2,1)S(1)} all-to-all(bf16[16,2,2304]{2,1,0:T(2,128)(2,1)S(1)} %reshape.625), channel_id=1, replica_groups=mesh['frame'=16,'within'=16] {'within'}, dimensions={0} | all-to-all | bytes 294912 | tf_op jit(solution)/shard_map/all_to_all | solution.py:12
  35.9 11.4 %all_to_all.121 = bf16[16,2,2304]{2,1,0:T(2,128)(2,1)S(1)} all-to-all(bf16[16,2,2304]{2,1,0:T(2,128)(2,1)S(1)} %reshape.621), channel_id=1, replica_groups=mesh['frame'=16,'within'=16] {'within'}, dimensions={0} | all-to-all | bytes 294912 | tf_op jit(solution)/shard_map/all_to_all | solution.py:13
  54.1 14.1 %all-to-all-start = ((bf16[16,2,2304]{2,1,0:T(2,128)(2,1)}), bf16[16,2,2304]{2,1,0:T(2,128)(2,1)S(1)}, u32[]{:S(2)}, u32[]{:S(2)}) async-start(bf16[16,2,2304]{2,1,0:T(2,128)(2,1)} %reshape.623), calls=%async_computation | async-start | bytes 294912 | tf_op jit(solution)/shard_map/all_to_all | solution.py:11
  76.6 9.3 %all-to-all-done = bf16[16,2,2304]{2,1,0:T(2,128)(2,1)S(1)} async-done(((bf16[16,2,2304]{2,1,0:T(2,128)(2,1)}), bf16[16,2,2304]{2,1,0:T(2,128)(2,1)S(1)}, u32[]{:S(2)}, u32[]{:S(2)}) %all-to-all-start) | async-done | bytes 147488 | tf_op jit(solution)/shard_map/all_to_all | solution.py:11
  86.0 3.5 all-to-all-start.2
  94.3 3.6 all-to-all-done.2
  103.4 3.6 fusion.2
  106.9 4.2 fusion.88
  111.2 4.2 fusion.87
  115.4 45.3 %all-gather.5.cloned.1.call-done = bf16[16,1152,64]{1,2,0:T(8,128)(2,1)} async-done(((bf16[1,1152,64]{1,2,0:T(8,128)(2,1)}), bf16[16,1152,64]{1,2,0:T(8,128)(2,1)}) %all-gather.5.cloned.1.call-update) | async-done | bytes 2359312 | tf_op jit(solution)/shard_map/all_gather | solution.py:85
  160.6 6.9 %fusion.3 = (f32[1152]{0:T(1024)S(1)}, f32[1152]{0:T(1024)S(1)}, f32[1152,1152]{0,1:T(8,128)}) fusion(f32[1152,1152]{0,1:T(8,128)} %get-tuple-element.98, f32[1152]{0:T(1024)S(1)} %get-tuple-element.97, bf16[1152,64]{0,1:T(8,128)(2,1)S(1)} %reshape.607, bf16[16,1152,64]{1,2,0:T(8,128)(2,1)} %all-gather.5.cloned.1.call-done, s32[]{:T(128)} %select_n.48), kind=kOutput, calls=%fused_computation.18 | convolution fusion | flops 175175424 | bytes 10926080 | tf_op jit(solution)/shard_map/qhd,khd->hqk/dot_general | solution.py:49
  167.5 5.6 %fusion.4 = (f32[1152]{0:T(1024)S(1)}, f32[1152]{0:T(1024)S(1)}, f32[1152,1152]{0,1:T(8,128)}) fusion(f32[1152,1152]{0,1:T(8,128)S(1)} %copy-done.3, f32[1152]{0:T(1024)S(1)} %get-tuple-element.94, bf16[1152,64]{0,1:T(8,128)(2,1)S(1)} %reshape.607, bf16[16,1152,64]{1,2,0:T(8,128)(2,1)} %all-gather.5.cloned.1.call-done, s32[]{:T(128)} %select_n.50), kind=kOutput, calls=%fused_computation.19 | convolution fusion | flops 175175424 | bytes 10926080 | tf_op jit(solution)/shard_map/qhd,khd->hqk/dot_general | solution.py:49
  173.2 8.1 %multiply_convert_fusion.1 = (bf16[1152,1152]{0,1:T(8,128)(2,1)S(1)}, bf16[1152,1152]{0,1:T(8,128)(2,1)S(1)}, bf16[1152,1152]{0,1:T(8,128)(2,1)S(1)}) fusion(f32[1152,1152]{0,1:T(8,128)} %get-tuple-element.101, f32[1152]{0:T(1024)S(1)} %get-tuple-element.84, f32[1152]{0:T(1024)S(1)} %get-tuple-element.83, f32[1152,1152]{0,1:T(8,128)S(1)} %bitcast.198, ...), kind=kLoop, calls=%fused_computation.6 | loop fusion | flops 19906560 | bytes 39826944 | tf_op jit(solution)/shard_map/convert_element_type | solution.py:67
  195.4 6.3 %fusion.20 = f32[16,1152,64]{1,2,0:T(8,128)} fusion(f32[16,1152,64]{1,2,0:T(8,128)} %broadcast_in_dim.64.clone.1, s32[]{:T(128)} %select_n.47, bf16[1152,64]{0,1:T(8,128)(2,1)S(1)} %reshape.607, f32[1152,1152]{0,1:T(8,128)} %copy-done.2, f32[1152]{0:T(1024)S(1)} %get-tuple-element.83, f32[1152]{0:T(1024)S(1)} %get-tuple-element.88, pred[]{:T(512)} %get-tuple-element.91), kind=kOutput, calls=%fused_computation.37 | convolution fusion | flops 173924352 | bytes 5761024 | tf_op jit(solution)/shard_map/hqk,qhd->khd/dot_general | solution.py:76
  201.7 3.5 fusion.32
  205.3 3.6 fusion.44
  215.2 6.7 %reduce.58 = bf16[1152,64]{1,0:T(8,128)(2,1)S(1)} reduce(bf16[1152,1,64]{2,1,0:T(2,128)(2,1)S(1)} %bitcast.202, bf16[]{:T(256)} %broadcast.338), dimensions={1}, to_apply=%bitcast.158.reduce_sub_computation | reduce | bytes 294914
  222.8 4.8 %all-to-all-start.4 = ((bf16[16,2,2304]{2,1,0:T(2,128)(2,1)}), bf16[16,2,2304]{2,1,0:T(2,128)(2,1)S(1)}, u32[]{:S(2)}, u32[]{:S(2)}) async-start(bf16[16,2,2304]{2,1,0:T(2,128)(2,1)} %reshape.627), calls=%async_computation.4 | async-start | bytes 294912 | tf_op jit(solution)/shard_map/all_to_all | solution.py:116
  227.5 71.0 %reduce-scatter.3.cloned.1.call-done = f32[1,1152,64]{1,2,0:T(8,128)} async-done(((f32[16,1152,64]{1,2,0:T(8,128)}), f32[1,1152,64]{1,2,0:T(8,128)}) %reduce-scatter.3.cloned.1.call-update) | async-done | bytes 294928 | tf_op jit(solution)/shard_map/reduce_scatter | solution.py:109
  300.3 6.7 %reduce.59 = bf16[1152,64]{1,0:T(8,128)(2,1)S(1)} reduce(bf16[1152,1,64]{2,1,0:T(2,128)(2,1)S(1)} %bitcast.203, bf16[]{:T(256)} %broadcast.338), dimensions={1}, to_apply=%bitcast.160.reduce_sub_computation | reduce | bytes 294914
  307.8 4.5 %all-to-all-start.5 = ((bf16[16,2,2304]{2,1,0:T(2,128)(2,1)}), bf16[16,2,2304]{2,1,0:T(2,128)(2,1)S(1)}, u32[]{:S(2)}, u32[]{:S(2)}) async-start(bf16[16,2,2304]{2,1,0:T(2,128)(2,1)} %reshape.629), calls=%async_computation.6 | async-start | bytes 294912 | tf_op jit(solution)/shard_map/all_to_all | solution.py:117
  312.3 95.1 %reduce-scatter.5.cloned.1.call-done = f32[1,1152,64]{1,2,0:T(8,128)} async-done(((f32[16,1152,64]{1,2,0:T(8,128)}), f32[1,1152,64]{1,2,0:T(8,128)}) %reduce-scatter.5.cloned.1.call-update) | async-done | bytes 294928 | tf_op jit(solution)/shard_map/reduce_scatter | solution.py:110
  409.1 6.7 %reduce.60 = bf16[1152,64]{1,0:T(8,128)(2,1)S(1)} reduce(bf16[1152,1,64]{2,1,0:T(2,128)(2,1)S(1)} %bitcast.201, bf16[]{:T(256)} %broadcast.338), dimensions={1}, to_apply=%bitcast.162.reduce_sub_computation | reduce | bytes 294914
  416.6 4.6 %all-to-all-start.6 = ((bf16[16,2,2304]{2,1,0:T(2,128)(2,1)}), bf16[16,2,2304]{2,1,0:T(2,128)(2,1)S(1)}, u32[]{:S(2)}, u32[]{:S(2)}) async-start(bf16[16,2,2304]{2,1,0:T(2,128)(2,1)} %reshape.631), calls=%async_computation.8 | async-start | bytes 294912 | tf_op jit(solution)/shard_map/all_to_all | solution.py:118
  (128 shorter events, 70.9 us)
Async XLA Ops:
  7.2 61.0 %copy-start = (s32[16,2]{0,1:T(2,128)S(1)}, s32[16,2]{0,1:T(2,128)}, u32[]{:S(2)}) copy-start(s32[16,2]{0,1:T(2,128)} %param.22) | copy-start | bytes 388
  7.2 43.0 %copy-start.7 = (bf16[1,72,1024]{2,1,0:T(8,128)(2,1)S(1)}, bf16[1,72,1024]{2,1,0:T(8,128)(2,1)}, u32[]{:S(2)}) copy-start(bf16[1,72,1024]{2,1,0:T(8,128)(2,1)} %param.18) | copy-start | bytes 442372
  7.2 99.7 %all-gather.3.cloned.1.call-start = ((), (), s32[]{:S(2)}) async-start(), calls=%async_computation.9 | async-start | bytes 2506752 | tf_op jit(solution)/shard_map/all_gather | solution.py:84
  11.8 59.2 %copy-start.8 = (bf16[1,72,1024]{2,1,0:T(8,128)(2,1)S(1)}, bf16[1,72,1024]{2,1,0:T(8,128)(2,1)}, u32[]{:S(2)}) copy-start(bf16[1,72,1024]{2,1,0:T(8,128)(2,1)} %param.21) | copy-start | bytes 442372
  30.2 45.8 %copy-start.9 = (s32[16]{0:T(128)S(1)}, s32[16]{0:T(128)}, u32[]{:S(2)}) copy-start(s32[16]{0:T(128)} %param.23) | copy-start | bytes 196
  30.4 60.3 %copy-start.10 = (s32[3]{0:T(128)S(1)}, s32[3]{0:T(128)}, u32[]{:S(2)}) copy-start(s32[3]{0:T(128)} %constant.142.clone.1) | copy-start | bytes 40
  31.8 128.8 %all-gather.5.cloned.1.call-start = ((), (), s32[]{:S(2)}) async-start(), calls=%async_computation.10 | async-start | bytes 2506752 | tf_op jit(solution)/shard_map/all_gather | solution.py:85
  54.1 31.9 %all-to-all-start = ((bf16[16,2,2304]{2,1,0:T(2,128)(2,1)}), bf16[16,2,2304]{2,1,0:T(2,128)(2,1)S(1)}, u32[]{:S(2)}, u32[]{:S(2)}) async-start(bf16[16,2,2304]{2,1,0:T(2,128)(2,1)} %reshape.623), calls=%async_computation | async-start | bytes 294912 | tf_op jit(solution)/shard_map/all_to_all | solution.py:11
  86.0 11.9 %all-to-all-start.2 = ((bf16[16,2,2304]{2,1,0:T(2,128)(2,1)}), bf16[16,2,2304]{2,1,0:T(2,128)(2,1)S(1)}, u32[]{:S(2)}, u32[]{:S(2)}) async-start(bf16[16,2,2304]{2,1,0:T(2,128)(2,1)} %reshape.619), calls=%async_computation.2 | async-start | bytes 294912 | tf_op jit(solution)/shard_map/all_to_all | solution.py:14
  89.5 209.1 %reduce-scatter.3.cloned.1.call-start = ((), (), s32[]{:S(2)}) async-start(), calls=%async_computation.11 | async-start | bytes 5013504 | tf_op jit(solution)/shard_map/reduce_scatter | solution.py:109
  160.6 6.9 %copy-start.3 = (f32[1152,1152]{0,1:T(8,128)S(1)}, f32[1152,1152]{0,1:T(8,128)}, u32[]{:S(2)}) copy-start(f32[1152,1152]{0,1:T(8,128)} %get-tuple-element.95) | copy-start | bytes 15925252
  160.6 12.6 %slice-start = ((s8[5308416]{0:T(1024)(128)(4,1)}), s8[4194304]{0:T(1024)(128)(4,1)S(1)}, s32[]{:S(2)}) async-start(s8[5308416]{0:T(1024)(128)(4,1)} %bitcast.193), calls=%async_computation.13 | async-start | bytes 8388608
  160.6 12.6 %slice-start.4 = ((s8[5308416]{0:T(1024)(128)(4,1)}), s8[4194304]{0:T(1024)(128)(4,1)S(1)}, s32[]{:S(2)}) async-start(s8[5308416]{0:T(1024)(128)(4,1)} %bitcast.197), calls=%async_computation.17 | async-start | bytes 8388608
  181.3 8.2 %copy-start.5 = (bf16[1152,1152]{0,1:T(8,128)(2,1)}, bf16[1152,1152]{0,1:T(8,128)(2,1)S(1)}, u32[]{:S(2)}) copy-start(bf16[1152,1152]{0,1:T(8,128)(2,1)S(1)} %get-tuple-element.85) | copy-start | bytes 7962628
  181.3 8.2 %copy-start.4 = (bf16[1152,1152]{0,1:T(8,128)(2,1)}, bf16[1152,1152]{0,1:T(8,128)(2,1)S(1)}, u32[]{:S(2)}) copy-start(bf16[1152,1152]{0,1:T(8,128)(2,1)S(1)} %get-tuple-element.86) | copy-start | bytes 7962628
  192.4 214.9 %reduce-scatter.5.cloned.1.call-start = ((), (), s32[]{:S(2)}) async-start(), calls=%async_computation.12 | async-start | bytes 5013504 | tf_op jit(solution)/shard_map/reduce_scatter | solution.py:110
  192.5 9.3 %slice-start.6 = ((s8[5308416]{0:T(1024)(128)(4,1)}), s8[4194304]{0:T(1024)(128)(4,1)S(1)}, s32[]{:S(2)}) async-start(s8[5308416]{0:T(1024)(128)(4,1)} %bitcast.199), calls=%async_computation.19 | async-start | bytes 8388608
  192.5 12.8 %slice-start.2 = ((s8[5308416]{0:T(1024)(128)(4,1)}), s8[4194304]{0:T(1024)(128)(4,1)S(1)}, s32[]{:S(2)}) async-start(s8[5308416]{0:T(1024)(128)(4,1)} %bitcast.195), calls=%async_computation.15 | async-start | bytes 8388608
  195.4 6.3 %slice-start.7 = ((s8[5308416]{0:T(1024)(128)(4,1)}), s8[1114112]{0:T(1024)(128)(4,1)S(1)}, s32[]{:S(2)}) async-start(s8[5308416]{0:T(1024)(128)(4,1)} %bitcast.199), calls=%async_computation.20 | async-start | bytes 2228224
  195.4 9.9 %slice-start.3 = ((s8[5308416]{0:T(1024)(128)(4,1)}), s8[1114112]{0:T(1024)(128)(4,1)S(1)}, s32[]{:S(2)}) async-start(s8[5308416]{0:T(1024)(128)(4,1)} %bitcast.195), calls=%async_computation.16 | async-start | bytes 2228224
  222.8 85.0 %all-to-all-start.4 = ((bf16[16,2,2304]{2,1,0:T(2,128)(2,1)}), bf16[16,2,2304]{2,1,0:T(2,128)(2,1)S(1)}, u32[]{:S(2)}, u32[]{:S(2)}) async-start(bf16[16,2,2304]{2,1,0:T(2,128)(2,1)} %reshape.627), calls=%async_computation.4 | async-start | bytes 294912 | tf_op jit(solution)/shard_map/all_to_all | solution.py:116
  307.8 108.8 %all-to-all-start.5 = ((bf16[16,2,2304]{2,1,0:T(2,128)(2,1)}), bf16[16,2,2304]{2,1,0:T(2,128)(2,1)S(1)}, u32[]{:S(2)}, u32[]{:S(2)}) async-start(bf16[16,2,2304]{2,1,0:T(2,128)(2,1)} %reshape.629), calls=%async_computation.6 | async-start | bytes 294912 | tf_op jit(solution)/shard_map/all_to_all | solution.py:117
  408.4 24.0 %copy-start.1 = (s32[16,2]{0,1:T(2,128)S(1)}, s32[16,2]{0,1:T(2,128)}, u32[]{:S(2)}) copy-start(s32[16,2]{0,1:T(2,128)} %param.22) | copy-start | bytes 388
  416.6 13.0 %all-to-all-start.6 = ((bf16[16,2,2304]{2,1,0:T(2,128)(2,1)}), bf16[16,2,2304]{2,1,0:T(2,128)(2,1)S(1)}, u32[]{:S(2)}, u32[]{:S(2)}) async-start(bf16[16,2,2304]{2,1,0:T(2,128)(2,1)} %reshape.631), calls=%async_computation.8 | async-start | bytes 294912 | tf_op jit(solution)/shard_map/all_to_all | solution.py:118
  (4 other events, 17.4 us)
Sparse Core Ops, SparseCore 0:
  31.9 59.9 all-gather.2
  94.7 65.9 all-gather.4
  192.6 105.9 reduce-scatter.2
  303.4 103.9 reduce-scatter.4
where the time goes:
time: 448 us; the launch traced here: 439 us
  waiting for transfers between devices  227 us (51%)
  matrix products  52.5 us (12%)
  other arithmetic  41.3 us (9%)
  local copies, waits for them, and re-layouts  39.8 us (9%)
  starting transfers between devices  31.6 us (7%)
  blocking collectives  28.5 us (6%)
  between operations  18.1 us (4%)
    reduce_scatter x1, waiting for transfers between devices, local(): lax.psum_scatter(results[2], 'frame', scatter_dimension=0, tiled=True)  95.1 us
    reduce_scatter x1, waiting for transfers between devices, local(): lax.psum_scatter(results[1], 'frame', scatter_dimension=0, tiled=True)  71 us
    all_gather x1, waiting for transfers between devices, local(): lax.all_gather(v_wide, 'frame', axis=0, tiled=True)  45.3 us
    unnamed x11, other arithmetic  29.2 us
    all_to_all x1, blocking collectives, local(): lax.all_to_all(keys_in, 'within', split_axis=2, concat_axis=1, tiled=True)  17.1 us
    unnamed x57, local copies, waits for them, and re-layouts  16.9 us
    all_to_all x1, starting transfers between devices, local(): lax.all_to_all(queries, 'within', split_axis=2, concat_axis=1, tiled=True)  14.1 us
    dot_general x3, matrix products, grads(): jnp.einsum('hqk,qhd->khd', prob_low, cotan3, preferred_element_type=jnp.f...  13.5 us
  transfers between devices with their start and end apart: 9, of which 6 were waited for; matrix products, arithmetic and copies ran while one was open for 19% of the time, Pallas kernels for 0%

commit v1 on v0

v1 whole, which is shorter than its diff:
```python
import jax
import jax.numpy as jnp
from jax import lax
from jax.experimental import pallas as pl
from jax.experimental.pallas import tpu as pltpu
from jax.sharding import PartitionSpec as P

DH = 64
HIDDEN_MOST = 288
BF16 = jnp.bfloat16
F32 = jnp.float32
VMEM = pl.BlockSpec(memory_space=pltpu.VMEM)
SMEM = pl.BlockSpec(memory_space=pltpu.SMEM)


def pair_up(low, high):
    return jnp.concatenate([low, high], axis=1)


def pack_kernel(q_ref, d_ref, k_ref, v_ref, out_ref):
    for pair in range(q_ref.shape[1] // (2 * DH)):
        cols = slice(2 * DH * pair, 2 * DH * (pair + 1))
        for place, (one, two) in enumerate(((q_ref, d_ref), (k_ref, v_ref))):
            a, b = one[:, cols], two[:, cols]
            lanes = slice(2 * DH * place, 2 * DH * (place + 1))
            out_ref[2 * pair, :, lanes] = pair_up(a[:, :DH], b[:, :DH])
            out_ref[2 * pair + 1, :, lanes] = pair_up(a[:, DH:], b[:, DH:])


def unpack_kernel(in_ref, q_ref, k_ref, v_ref):
    for pair in range(q_ref.shape[1] // (2 * DH)):
        cols = slice(2 * DH * pair, 2 * DH * (pair + 1))
        for place, out in enumerate((k_ref, v_ref, q_ref)):
            lanes = slice(DH * place, DH * (place + 1))
            out[:, cols] = pair_up(in_ref[2 * pair, :, lanes], in_ref[2 * pair + 1, :, lanes])


def pick_kernel(partners_ref, in_ref, out_ref):
    for group in range(in_ref.shape[0]):
        for slot in range(2):
            other = partners_ref[group, slot]
            out_ref[group, :, 128 * slot : 128 * (slot + 1)] = in_ref[other, :, 128:256]


def sum_kernel(partners_ref, own_ref, listed_ref, out_ref, total):
    groups = own_ref.shape[0]
    for group in range(groups):
        total[group] = own_ref[group, :, 0:128].astype(F32)
    for group in range(groups):
        for slot in range(2):
            other = partners_ref[group, slot]
            total[other] += listed_ref[group, :, 128 * slot : 128 * (slot + 1)].astype(F32)
    for group in range(groups):
        out_ref[group, :, 0:128] = total[group].astype(BF16)
        out_ref[group, :, 128:256] = own_ref[group, :, 128:256]


def attend_kernel(hidden_ref, own_ref, listed_ref, own_out, listed_out, kv, kt, s_ref, dp_ref, total):
    seq = own_ref.shape[0]
    kv[0] = own_ref[:, 128:256]
    kv[1] = listed_ref[:, 0:128]
    kv[2] = listed_ref[:, 128:256]
    for j in range(3):
        kt[j] = kv[j].T[:DH, :]
    total[...] = jnp.zeros_like(total)

    def tile(start, size):
        rows = pl.ds(start, size)
        qd = own_ref[rows, 0:128]
        left = lax.broadcasted_iota(jnp.int32, qd.shape, 1) < DH
        q_only = jnp.where(left, qd.astype(F32) * 0.125, 0.0).astype(BF16)
        d_only = jnp.where(left, 0.0, qd.astype(F32)).astype(BF16)
        nt = (((1,), (1,)), ((), ()))
        top = jnp.full((1, size), -jnp.inf, F32)
        for j in range(3):
            raw = lax.dot_general(kv[j], q_only, nt, preferred_element_type=F32)
            if j:
                head = raw[:HIDDEN_MOST]
                place = lax.broadcasted_iota(jnp.int32, head.shape, 0)
                head = jnp.where(place >= hidden_ref[j - 1], head, -1e30)
                raw = jnp.concatenate([head, raw[HIDDEN_MOST:]], axis=0)
            s_ref[j, :, :size] = raw
            top = jnp.maximum(top, jnp.max(raw, axis=0, keepdims=True))
        norm = jnp.zeros((1, size), F32)
        dsum = jnp.zeros((1, size), F32)
        for j in range(3):
            expo = jnp.exp(s_ref[j, :, :size] - top)
            dprod = lax.dot_general(kv[j], d_only, nt, preferred_element_type=F32)
            s_ref[j, :, :size] = expo
            dp_ref[j, :, :size] = dprod
            norm += jnp.sum(expo, axis=0, keepdims=True)
            dsum += jnp.sum(expo * dprod, axis=0, keepdims=True)
        inv = 1.0 / norm
        delta = dsum * inv
        dq = jnp.zeros((DH, size), F32)
        for j in range(3):
            prob = s_ref[j, :, :size] * inv
            dscore = (prob * (dp_ref[j, :, :size] - delta)).astype(BF16)
            prob = prob.astype(BF16)
            total[j] += jnp.dot(dscore, q_only, preferred_element_type=F32) + jnp.dot(
                prob, d_only, preferred_element_type=F32
            )
            dq += jnp.dot(kt[j], dscore, preferred_element_type=F32)
        dq = (dq * 0.125).T
        own_out[rows, 128:256] = pair_up(dq, jnp.zeros_like(dq)).astype(BF16)

    wide = 256

    @pl.loop(0, seq // wide)
    def _(i):
        tile(pl.multiple_of(i * wide, wide), wide)

    if seq % wide:
        tile(seq // wide * wide, seq % wide)
    own_out[:, 0:128] = total[0].astype(BF16)
    listed_out[:, 0:128] = total[1].astype(BF16)
    listed_out[:, 128:256] = total[2].astype(BF16)


def shape(*dims):
    return jax.ShapeDtypeStruct(dims, BF16)


def attend(hidden, own, listed):
    seq = own.shape[0]
    return pl.pallas_call(
        attend_kernel,
        out_shape=(shape(seq, 256), shape(seq, 256)),
        in_specs=[SMEM, VMEM, VMEM],
        out_specs=(VMEM, VMEM),
        scratch_shapes=[
            pltpu.VMEM((3, seq, 128), BF16),
            pltpu.VMEM((3, DH, seq), BF16),
            pltpu.VMEM((3, seq, 256), F32),
            pltpu.VMEM((3, seq, 256), F32),
            pltpu.VMEM((3, seq, 128), F32),
        ],
        compiler_params=pltpu.CompilerParams(vmem_limit_bytes=48 * 2**20),
        cost_estimate=pl.CostEstimate(flops=2 * 15 * seq * seq * DH, bytes_accessed=4 * seq * 512, transcendentals=3 * seq * seq),
        name="attend",
    )(hidden, own, listed)


def local(queries, keys_in, values_in, grad_out, partners, registers):
    rows, width = queries.shape[1:]
    heads = width // DH
    groups = partners.shape[0]
    small = pltpu.CompilerParams(vmem_limit_bytes=32 * 2**20)
    packed = pl.pallas_call(
        pack_kernel, out_shape=shape(heads, rows, 256), in_specs=[VMEM] * 4, out_specs=VMEM, name="pack", compiler_params=small
    )(queries[0], grad_out[0], keys_in[0], values_in[0])
    by_group = lax.all_to_all(packed, "frame", 0, 0, tiled=True)
    picked = pl.pallas_call(
        pick_kernel, out_shape=shape(groups, rows, 256), in_specs=[SMEM, VMEM], out_specs=VMEM, name="pick", compiler_params=small
    )(partners, by_group)
    own = lax.all_to_all(by_group, "within", 0, 0, tiled=True)
    listed = lax.all_to_all(picked, "within", 0, 0, tiled=True)
    hidden = registers[partners[lax.axis_index("within")]]
    seq = rows * own.shape[0]
    own_out, listed_out = attend(hidden, own.reshape(seq, 256), listed.reshape(seq, 256))
    own_out = lax.all_to_all(own_out.reshape(own.shape), "within", 0, 0, tiled=True)
    listed_out = lax.all_to_all(listed_out.reshape(own.shape), "within", 0, 0, tiled=True)
    summed = pl.pallas_call(
        sum_kernel,
        out_shape=shape(groups, rows, 256),
        in_specs=[SMEM, VMEM, VMEM],
        out_specs=VMEM,
        scratch_shapes=[pltpu.VMEM((groups, rows, 128), F32)],
        name="sum",
        compiler_params=small,
    )(partners, own_out, listed_out)
    by_head = lax.all_to_all(summed, "frame", 0, 0, tiled=True)
    dq, dk, dv = pl.pallas_call(
        unpack_kernel, out_shape=(shape(rows, width),) * 3, in_specs=[VMEM], out_specs=(VMEM,) * 3, name="unpack", compiler_params=small
    )(by_head)
    return dq[None], dk[None], dv[None]


def solution(mesh):
    tokens = P("frame", "within", None)
    return jax.shard_map(
        local,
        mesh=mesh,
        in_specs=(tokens,) * 4 + (P(), P()),
        out_specs=(tokens,) * 3,
        check_vma=False,
    )
```

time: 448 us -> 165 us (0.37)
  the two profiles are of different devices: /device:TPU:2 before, /device:TPU:1 now
where the time goes in v1:
time: 165 us; the launch traced here: 162 us
  blocking collectives  90.9 us (55%)
  waiting for transfers between devices  31.3 us (19%)
  Pallas kernels  19.7 us (12%)
  starting transfers between devices  14.6 us (9%)
  local copies, waits for them, and re-layouts  4.56 us (3%)
    all_to_all x1, blocking collectives, local(): by_group = lax.all_to_all(packed, 'frame', 0, 0, tiled=True)  28.6 us
    all_to_all x1, blocking collectives, local(): by_head = lax.all_to_all(summed, 'frame', 0, 0, tiled=True)  21.3 us
    all_to_all x1, blocking collectives, local(): lax.all_to_all(own_out.reshape(own.shape), 'within', 0, 0, tiled=True)  20.6 us
    all_to_all x1, blocking collectives, local(): lax.all_to_all(listed_out.reshape(own.shape), 'within', 0, 0, tiled=True)  20.4 us
    all_to_all x1, waiting for transfers between devices, local(): listed = lax.all_to_all(picked, 'within', 0, 0, tiled=True)  16.3 us
    pallas_call x1, Pallas kernels, attend(): pl.pallas_call(attend_kernel, out_shape=(shape(seq, 256), shape(seq, 256)...  15.6 us
    all_to_all x1, waiting for transfers between devices, local(): own = lax.all_to_all(by_group, 'within', 0, 0, tiled=True)  15 us
    all_to_all x1, starting transfers between devices, local(): own = lax.all_to_all(by_group, 'within', 0, 0, tiled=True)  10.5 us
  transfers between devices with their start and end apart: 2, of which 2 were waited for; matrix products, arithmetic and copies ran while one was open for 1% of the time, Pallas kernels for 1%

profile of v1, /device:TPU:1, one launch (start us, length us, event | category | flops | bytes accessed | tf_op | source)
XLA Modules:
  0.0 161.9 jit_solution(5895113738993486151)
XLA Ops:
  0.6 0.0 copy-start
  0.6 0.0 copy-start.1
  0.7 0.9 copy-done.1
  1.6 0.9 copy-done.2
  2.5 0.9 copy-done.3
  3.4 0.9 copy-done.4
  4.3 0.2 pack.1
  4.5 28.6 %all_to_all.30.in_ref = bf16[16,72,256]{2,1,0:T(8,128)(2,1)} all-to-all(bf16[16,72,256]{2,1,0:T(8,128)(2,1)S(1)} %pack.1), channel_id=1, replica_groups=mesh['frame'=16,'within'=16] {'frame'}, dimensions={0} | all-to-all | bytes 1179648 | tf_op jit(solution)/shard_map/all_to_all | solution.py:152
  33.2 10.5 %all-to-all-start.1 = ((bf16[16,72,256]{2,1,0:T(8,128)(2,1)}), bf16[16,72,256]{2,1,0:T(8,128)(2,1)S(1)}, u32[]{:S(2)}, u32[]{:S(2)}) async-start(bf16[16,72,256]{2,1,0:T(8,128)(2,1)} %all_to_all.30.in_ref), calls=%async_computation.1 | async-start | bytes 1179648 | tf_op jit(solution)/shard_map/all_to_all | solution.py:156
  43.7 0.0 copy-done.5
  43.7 0.1 copy.12.partners_ref
  43.8 2.0 %pick.1 = bf16[16,72,256]{2,1,0:T(8,128)(2,1)} custom-call(s32[16,2]{1,0:T(8,128)S(1)} %copy.12.partners_ref, bf16[16,72,256]{2,1,0:T(8,128)(2,1)} %all_to_all.30.in_ref), custom_call_target="tpu_custom_call" | custom-call | tf_op jit(solution)/shard_map/pick/pallas_call | solution.py:153
  45.8 15.0 %all-to-all-done.1 = bf16[16,72,256]{2,1,0:T(8,128)(2,1)S(1)} async-done(((bf16[16,72,256]{2,1,0:T(8,128)(2,1)}), bf16[16,72,256]{2,1,0:T(8,128)(2,1)S(1)}, u32[]{:S(2)}, u32[]{:S(2)}) %all-to-all-start.1) | async-done | bytes 589856 | tf_op jit(solution)/shard_map/all_to_all | solution.py:156
  60.9 4.1 %all-to-all-start.2 = ((bf16[16,72,256]{2,1,0:T(8,128)(2,1)}), bf16[16,72,256]{2,1,0:T(8,128)(2,1)S(1)}, u32[]{:S(2)}, u32[]{:S(2)}) async-start(bf16[16,72,256]{2,1,0:T(8,128)(2,1)} %pick.1), calls=%async_computation.2 | async-start | bytes 1179648 | tf_op jit(solution)/shard_map/all_to_all | solution.py:157
  65.0 0.2 dynamic-slice_reduce_fusion
  65.2 0.0 copy-done
  65.2 0.6 gather_fusion
  65.8 16.3 %all-to-all-done.2 = bf16[16,72,256]{2,1,0:T(8,128)(2,1)S(1)} async-done(((bf16[16,72,256]{2,1,0:T(8,128)(2,1)}), bf16[16,72,256]{2,1,0:T(8,128)(2,1)S(1)}, u32[]{:S(2)}, u32[]{:S(2)}) %all-to-all-start.2) | async-done | bytes 589856 | tf_op jit(solution)/shard_map/all_to_all | solution.py:157
  82.1 15.6 %attend.1 = (bf16[1152,256]{1,0:T(8,128)(2,1)S(1)}, bf16[1152,256]{1,0:T(8,128)(2,1)S(1)}) custom-call(s32[2]{0:T(128)S(1)} %gather_fusion, bf16[1152,256]{1,0:T(8,128)(2,1)S(1)} %bitcast.15, bf16[1152,256]{1,0:T(8,128)(2,1)S(1)} %bitcast.16), custom_call_target="tpu_custom_call" | custom-call | flops 2548039680 | bytes 2359296 | tf_op jit(solution)/shard_map/attend/pallas_call | solution.py:126
  97.7 20.4 %all_to_all.31.listed_ref = bf16[16,72,256]{2,1,0:T(8,128)(2,1)S(1)} all-to-all(bf16[16,72,256]{2,1,0:T(8,128)(2,1)S(1)} %bitcast.18), channel_id=1, replica_groups=mesh['frame'=16,'within'=16] {'within'}, dimensions={0} | all-to-all | bytes 1179648 | tf_op jit(solution)/shard_map/all_to_all | solution.py:162
  118.1 20.6 %all_to_all.32.own_ref = bf16[16,72,256]{2,1,0:T(8,128)(2,1)S(1)} all-to-all(bf16[16,72,256]{2,1,0:T(8,128)(2,1)S(1)} %bitcast.17), channel_id=1, replica_groups=mesh['frame'=16,'within'=16] {'within'}, dimensions={0} | all-to-all | bytes 1179648 | tf_op jit(solution)/shard_map/all_to_all | solution.py:161
  138.7 1.0 sum.1
  139.6 21.3 %all_to_all.33.in_ref = bf16[16,72,256]{2,1,0:T(8,128)(2,1)S(1)} all-to-all(bf16[16,72,256]{2,1,0:T(8,128)(2,1)S(1)} %sum.1), channel_id=1, replica_groups=mesh['frame'=16,'within'=16] {'frame'}, dimensions={0} | all-to-all | bytes 1179648 | tf_op jit(solution)/shard_map/all_to_all | solution.py:172
  160.9 0.9 unpack.1
  (6 shorter events, 0.0 us)
Async XLA Ops:
  0.6 64.6 %copy-start = (s32[16]{0:T(128)S(1)}, s32[16]{0:T(128)}, u32[]{:S(2)}) copy-start(s32[16]{0:T(128)} %param.11) | copy-start | bytes 196
  0.6 0.9 copy-start.1
  1.6 0.9 copy-start.2
  2.5 0.9 copy-start.3
  3.4 0.9 copy-start.4
  33.2 10.5 %copy-start.5 = (s32[16,2]{0,1:T(2,128)S(1)}, s32[16,2]{0,1:T(2,128)}, u32[]{:S(2)}) copy-start(s32[16,2]{0,1:T(2,128)} %param.10) | copy-start | bytes 388
  33.2 27.7 %all-to-all-start.1 = ((bf16[16,72,256]{2,1,0:T(8,128)(2,1)}), bf16[16,72,256]{2,1,0:T(8,128)(2,1)S(1)}, u32[]{:S(2)}, u32[]{:S(2)}) async-start(bf16[16,72,256]{2,1,0:T(8,128)(2,1)} %all_to_all.30.in_ref), calls=%async_computation.1 | async-start | bytes 1179648 | tf_op jit(solution)/shard_map/all_to_all | solution.py:156
  60.9 21.2 %all-to-all-start.2 = ((bf16[16,72,256]{2,1,0:T(8,128)(2,1)}), bf16[16,72,256]{2,1,0:T(8,128)(2,1)S(1)}, u32[]{:S(2)}, u32[]{:S(2)}) async-start(bf16[16,72,256]{2,1,0:T(8,128)(2,1)} %pick.1), calls=%async_computation.2 | async-start | bytes 1179648 | tf_op jit(solution)/shard_map/all_to_all | solution.py:157

commit v2 on v1

v2 whole, which is shorter than its diff:
```python
import jax
import jax.numpy as jnp
import numpy as np
from jax import lax
from jax.experimental import pallas as pl
from jax.experimental.pallas import tpu as pltpu
from jax.sharding import Mesh
from jax.sharding import PartitionSpec as P

DH = 64
HALF = DH // 2
HIDDEN_MOST = 288
BF16 = jnp.bfloat16
F32 = jnp.float32
VMEM = pl.BlockSpec(memory_space=pltpu.VMEM)
SMEM = pl.BlockSpec(memory_space=pltpu.SMEM)

FINE = (("zh", 2), ("x1", 2), ("x0", 2), ("c", 2), ("y", 4), ("zl1", 2), ("zl0", 2))
OUTER = ("zh", "x1", "x0", "c", "zl1")
INNER = ("y", "x0", "zl0")


def piece(head, half):
    return head // 4 * 8 + half * 4 + head % 4


def columns(head, half):
    return slice(DH * head + HALF * half, DH * head + HALF * (half + 1))


def pack_kernel(q_ref, d_ref, k_ref, v_ref, out_ref):
    for head in range(q_ref.shape[1] // DH):
        for half in range(2):
            parts = [ref[:, columns(head, half)] for ref in (q_ref, d_ref, k_ref, v_ref)]
            out_ref[piece(head, half)] = jnp.concatenate(parts, axis=1)


def unpack_kernel(in_ref, q_ref, k_ref, v_ref):
    for pair in range(q_ref.shape[1] // (2 * DH)):
        for out, place in ((q_ref, 0), (k_ref, 2), (v_ref, 3)):
            lanes = slice(HALF * place, HALF * (place + 1))
            parts = [in_ref[piece(2 * pair + i // 2, i % 2)][:, lanes] for i in range(4)]
            out[:, 2 * DH * pair : 2 * DH * (pair + 1)] = jnp.concatenate(parts, axis=1)


def pick_kernel(partners_ref, in_ref, out_ref):
    for group in range(in_ref.shape[0]):
        out_ref[group, :, 0:128] = in_ref[group]
        one, two = in_ref[partners_ref[group, 0]], in_ref[partners_ref[group, 1]]
        out_ref[group, :, 128:256] = jnp.concatenate([one[:, DH:], two[:, DH:]], axis=1)


def sum_kernel(partners_ref, in_ref, out_ref, total):
    groups = in_ref.shape[0]
    for group in range(groups):
        total[group] = in_ref[group, :, 0:128].astype(F32)
    left = lax.broadcasted_iota(jnp.int32, total.shape[1:], 1) < DH
    for group in range(groups):
        listed = in_ref[group, :, 128:256].astype(F32)
        one, two = partners_ref[group, 0], partners_ref[group, 1]
        total[one] += jnp.where(left, 0.0, pltpu.roll(listed, DH, 1))
        total[two] += jnp.where(left, 0.0, listed)
    for group in range(groups):
        out_ref[group] = total[group].astype(BF16)


WIDE = 256


def attend_kernel(hidden_ref, in_ref, out_ref, own, listed, kt, bias, s_ref, dp_ref, total):
    sources, rows_of = in_ref.shape[:2]
    seq = own.shape[0]
    blocks = [(s // 4 * 2 + s % 2, s // 2 % 2) for s in range(sources)]
    for source, (block, half) in enumerate(blocks):
        rows = slice(block * rows_of, (block + 1) * rows_of)
        lanes = slice(128 * half, 128 * (half + 1))
        own[rows, lanes] = in_ref[source, :, 0:128]
        listed[rows, lanes] = in_ref[source, :, 128:256]
    for j, (keys, place) in enumerate(((own, DH), (listed, 0), (listed, DH))):
        both = keys[...].T
        kt[j] = jnp.concatenate([both[place : place + HALF], both[128 + place : 128 + place + HALF]], axis=0)
    index = lax.broadcasted_iota(jnp.int32, bias.shape[1:], 0)
    chunk = rows_of // 2
    swap = (index >= chunk) & (index < 3 * chunk)
    place = jnp.where(swap, jnp.where(index < 2 * chunk, index + chunk, index - chunk), index)
    for j in range(2):
        bias[j] = jnp.where(place >= hidden_ref[j], 0.0, -1e30)
    total[...] = jnp.zeros_like(total)
    nt = (((1,), (1,)), ((), ()))

    def tile(start, size):
        rows = pl.ds(start, size)
        x = own[rows, :].astype(F32)
        lane = lax.broadcasted_iota(jnp.int32, x.shape, 1) % 128
        turned = jnp.concatenate([pltpu.roll(x[:, :128], DH, 1), pltpu.roll(x[:, 128:], DH, 1)], axis=1)
        q_low = jnp.where(lane < HALF, x * 0.125, 0.0).astype(BF16)
        d_low = jnp.where((lane >= HALF) & (lane < DH), x, 0.0).astype(BF16)
        q_high = jnp.where((lane >= DH) & (lane < DH + HALF), turned * 0.125, 0.0).astype(BF16)
        d_high = jnp.where(lane >= DH + HALF, turned, 0.0).astype(BF16)
        terms = ((own, q_high, d_high), (listed, q_low, d_low), (listed, q_high, d_high))
        top = jnp.full((1, size), -jnp.inf, F32)
        for j, (keys, q_side, _) in enumerate(terms):
            raw = lax.dot_general(keys[...], q_side, nt, preferred_element_type=F32)
            if j:
                head = raw[:HIDDEN_MOST] + bias[j - 1, :, :size]
                raw = jnp.concatenate([head, raw[HIDDEN_MOST:]], axis=0)
            s_ref[j, :, :size] = raw
            top = jnp.maximum(top, jnp.max(raw, axis=0, keepdims=True))
        norm = jnp.zeros((1, size), F32)
        dsum = jnp.zeros((1, size), F32)
        for j, (keys, _, d_side) in enumerate(terms):
            expo = jnp.exp(s_ref[j, :, :size] - top)
            dprod = lax.dot_general(keys[...], d_side, nt, preferred_element_type=F32)
            s_ref[j, :, :size] = expo
            dp_ref[j, :, :size] = dprod
            norm += jnp.sum(expo, axis=0, keepdims=True)
            dsum += jnp.sum(expo * dprod, axis=0, keepdims=True)
        inv = 1.0 / norm
        delta = dsum * inv
        dq = jnp.zeros((DH, size), F32)
        for j, (_, q_side, d_side) in enumerate(terms):
            prob = s_ref[j, :, :size] * inv
            dscore = (prob * (dp_ref[j, :, :size] - delta)).astype(BF16)
            both = jnp.concatenate([dscore, prob.astype(BF16)], axis=1)
            sides = jnp.concatenate([q_side, d_side], axis=0)
            total[min(j, 1)] += jnp.dot(both, sides, preferred_element_type=F32)
            dq += jnp.dot(kt[j], dscore, preferred_element_type=F32)
        dq = dq * 0.125
        gap = jnp.zeros((128 - HALF, size), F32)
        total[0, rows, :] += jnp.concatenate([dq[:HALF], gap, dq[HALF:], gap], axis=0).T

    @pl.loop(0, seq // WIDE)
    def _(i):
        tile(pl.multiple_of(i * WIDE, WIDE), WIDE)

    if seq % WIDE:
        tile(seq // WIDE * WIDE, seq % WIDE)
    for source, (block, half) in enumerate(blocks):
        rows = slice(block * rows_of, (block + 1) * rows_of)
        lanes = slice(128 * half, 128 * (half + 1))
        out_ref[source, :, 0:128] = total[0, rows, lanes].astype(BF16)
        out_ref[source, :, 128:256] = total[1, rows, lanes].astype(BF16)


def shape(*dims):
    return jax.ShapeDtypeStruct(dims, BF16)


def attend(hidden, rows):
    seq = rows.shape[0] * rows.shape[1] // 2
    return pl.pallas_call(
        attend_kernel,
        out_shape=shape(*rows.shape),
        in_specs=[SMEM, VMEM],
        out_specs=VMEM,
        scratch_shapes=[
            pltpu.VMEM((seq, 256), BF16),
            pltpu.VMEM((seq, 256), BF16),
            pltpu.VMEM((3, DH, seq), BF16),
            pltpu.VMEM((2, HIDDEN_MOST, WIDE), F32),
            pltpu.VMEM((3, seq, WIDE), F32),
            pltpu.VMEM((3, seq, WIDE), F32),
            pltpu.VMEM((2, seq, 256), F32),
        ],
        compiler_params=pltpu.CompilerParams(vmem_limit_bytes=48 * 2**20),
        name="attend",
    )(hidden, rows)


def local(queries, keys_in, values_in, grad_out, partners, registers):
    rows, width = queries.shape[1:]
    groups = partners.shape[0]
    pieces = 2 * width // DH
    small = pltpu.CompilerParams(vmem_limit_bytes=32 * 2**20)
    packed = pl.pallas_call(
        pack_kernel, out_shape=shape(pieces, rows, 128), in_specs=[VMEM] * 4, out_specs=VMEM, name="pack", compiler_params=small
    )(queries[0], grad_out[0], keys_in[0], values_in[0])
    by_group = lax.all_to_all(packed, OUTER, 0, 0, tiled=True).reshape(groups, 2 * rows, 128)
    picked = pl.pallas_call(
        pick_kernel, out_shape=shape(groups, 2 * rows, 256), in_specs=[SMEM, VMEM], out_specs=VMEM, name="pick", compiler_params=small
    )(partners, by_group)
    gathered = lax.all_to_all(picked, INNER, 0, 0, tiled=True)
    hidden = registers[partners[lax.axis_index(INNER)]]
    spread = lax.all_to_all(attend(hidden, gathered), INNER, 0, 0, tiled=True)
    summed = pl.pallas_call(
        sum_kernel,
        out_shape=shape(groups, 2 * rows, 128),
        in_specs=[SMEM, VMEM],
        out_specs=VMEM,
        scratch_shapes=[pltpu.VMEM((groups, 2 * rows, 128), F32)],
        name="sum",
        compiler_params=small,
    )(partners, spread)
    by_head = lax.all_to_all(summed.reshape(pieces, rows, 128), OUTER, 0, 0, tiled=True)
    dq, dk, dv = pl.pallas_call(
        unpack_kernel, out_shape=(shape(rows, width),) * 3, in_specs=[VMEM], out_specs=(VMEM,) * 3, name="unpack", compiler_params=small
    )(by_head)
    return dq[None], dk[None], dv[None]


def solution(mesh):
    names = tuple(name for name, _ in FINE)
    fine = Mesh(np.asarray(mesh.devices).reshape([size for _, size in FINE]), names)
    tokens = P(names[:4], names[4:], None)
    return jax.shard_map(
        local,
        mesh=fine,
        in_specs=(tokens,) * 4 + (P(), P()),
        out_specs=(tokens,) * 3,
        check_vma=False,
    )
```

time: 165 us -> 129 us (0.78); the launches traced: 162 us -> 129 us
  blocking collectives: 90.9 us -> 50.3 us
  starting transfers between devices: 14.6 us -> 18.5 us
  Pallas kernels: 19.7 us -> 23.2 us
    all_to_all x4 -> x2, blocking collectives: 90.9 us -> 50.3 us  [the longest x1 32 us: local(): lax.all_to_all(summed.reshape(pieces, rows, 128), OUTER, 0, 0, tiled=True)]
    all_to_all x2, starting transfers between devices: 14.6 us -> 18.5 us  [the longest x1 12.6 us: local(): lax.all_to_all(packed, OUTER, 0, 0, tiled=True)]
    pallas_call x4, Pallas kernels: 18.8 us -> 22 us  [the longest x1 17.4 us: attend(): pl.pallas_call(attend_kernel, out_shape=shape(*rows.shape), in_specs=[SME...]
  transfers between devices with their start and end apart: 2 -> 2, of which waited for: 2 -> 2; matrix products, arithmetic and copies ran while one was open for 1% -> 1% of each run, Pallas kernels for 1% -> 0%
where the time goes in v2:
time: 129 us
  blocking collectives  50.3 us (39%)
  waiting for transfers between devices  31.9 us (25%)
  Pallas kernels  23.2 us (18%)
  starting transfers between devices  18.5 us (14%)
  local copies, waits for them, and re-layouts  4.56 us (4%)
    all_to_all x1, blocking collectives, local(): lax.all_to_all(summed.reshape(pieces, rows, 128), OUTER, 0, 0, tiled=True)  32 us
    all_to_all x1, blocking collectives, local(): spread = lax.all_to_all(attend(hidden, gathered), INNER, 0, 0, tiled=True)  18.2 us
    all_to_all x1, waiting for transfers between devices, local(): lax.all_to_all(packed, OUTER, 0, 0, tiled=True)  17.8 us
    pallas_call x1, Pallas kernels, attend(): pl.pallas_call(attend_kernel, out_shape=shape(*rows.shape), in_specs=[SME...  17.4 us
    all_to_all x1, waiting for transfers between devices, local(): gathered = lax.all_to_all(picked, INNER, 0, 0, tiled=True)  14 us
    all_to_all x1, starting transfers between devices, local(): lax.all_to_all(packed, OUTER, 0, 0, tiled=True)  12.6 us
    all_to_all x1, starting transfers between devices, local(): gathered = lax.all_to_all(picked, INNER, 0, 0, tiled=True)  5.87 us
    unnamed x13, local copies, waits for them, and re-layouts  3.73 us
  transfers between devices with their start and end apart: 2, of which 2 were waited for; matrix products, arithmetic and copies ran while one was open for 1% of the time, Pallas kernels for 0%

profile of v2, /device:TPU:1, one launch (start us, length us, event | category | flops | bytes accessed | tf_op | source)
XLA Modules:
  0.0 129.0 jit_solution(5762940610241424288)
XLA Ops:
  0.6 0.0 copy-start
  0.6 0.0 copy-start.1
  0.7 0.9 copy-done.1
  1.6 0.0 copy-start.2
  1.6 0.9 copy-done.2
  2.5 0.0 copy-start.3
  2.5 0.9 copy-done.3
  3.4 0.9 copy-done.4
  4.3 1.4 %pack.1 = bf16[32,72,128]{2,1,0:T(8,128)(2,1)} custom-call(bf16[72,1024]{1,0:T(8,128)(2,1)S(1)} %bitcast.15, bf16[72,1024]{1,0:T(8,128)(2,1)S(1)} %bitcast.16, bf16[72,1024]{1,0:T(8,128)(2,1)S(1)} %bitcast.17, bf16[72,1024]{1,0:T(8,128)(2,1)S(1)} %bitcast.18), custom_call_target="tpu_custom_call" | custom-call | tf_op jit(solution)/shard_map/pack/pallas_call | solution.py:175
  5.7 12.6 %all-to-all-start = ((bf16[32,72,128]{2,1,0:T(8,128)(2,1)}), bf16[32,72,128]{2,1,0:T(8,128)(2,1)S(1)}, u32[]{:S(2)}, u32[]{:S(2)}) async-start(bf16[32,72,128]{2,1,0:T(8,128)(2,1)} %pack.1), calls=%async_computation | async-start | bytes 1179648 | tf_op jit(solution)/shard_map/all_to_all | solution.py:178
  18.3 0.0 copy-done.5
  18.3 0.1 copy.12.partners_ref
  18.4 17.8 %all-to-all-done = bf16[32,72,128]{2,1,0:T(8,128)(2,1)S(1)} async-done(((bf16[32,72,128]{2,1,0:T(8,128)(2,1)}), bf16[32,72,128]{2,1,0:T(8,128)(2,1)S(1)}, u32[]{:S(2)}, u32[]{:S(2)}) %all-to-all-start) | async-done | bytes 589856 | tf_op jit(solution)/shard_map/all_to_all | solution.py:178
  36.2 2.0 %pick.1 = bf16[16,144,256]{2,1,0:T(8,128)(2,1)} custom-call(s32[16,2]{1,0:T(8,128)S(1)} %copy.12.partners_ref, bf16[16,144,128]{2,1,0:T(8,128)(2,1)S(1)} %bitcast.13), custom_call_target="tpu_custom_call" | custom-call | tf_op jit(solution)/shard_map/pick/pallas_call | solution.py:179
  38.2 5.9 %all-to-all-start.1 = ((bf16[16,144,256]{2,1,0:T(8,128)(2,1)}), bf16[16,144,256]{2,1,0:T(8,128)(2,1)S(1)}, u32[]{:S(2)}, u32[]{:S(2)}) async-start(bf16[16,144,256]{2,1,0:T(8,128)(2,1)} %pick.1), calls=%async_computation.1 | async-start | bytes 2359296 | tf_op jit(solution)/shard_map/all_to_all | solution.py:182
  44.1 0.2 dynamic-slice_reduce_fusion
  44.3 0.0 copy-done
  44.3 0.6 gather_fusion
  44.9 14.0 %all-to-all-done.1.in_ref = bf16[16,144,256]{2,1,0:T(8,128)(2,1)S(1)} async-done(((bf16[16,144,256]{2,1,0:T(8,128)(2,1)}), bf16[16,144,256]{2,1,0:T(8,128)(2,1)S(1)}, u32[]{:S(2)}, u32[]{:S(2)}) %all-to-all-start.1) | async-done | bytes 1179680 | tf_op jit(solution)/shard_map/all_to_all | solution.py:182
  59.0 17.4 %attend.1 = bf16[16,144,256]{2,1,0:T(8,128)(2,1)S(1)} custom-call(s32[2]{0:T(128)S(1)} %gather_fusion, bf16[16,144,256]{2,1,0:T(8,128)(2,1)S(1)} %all-to-all-done.1.in_ref), custom_call_target="tpu_custom_call" | custom-call | tf_op jit(solution)/shard_map/attend/pallas_call | solution.py:151
  76.4 18.2 %all_to_all.20.in_ref = bf16[16,144,256]{2,1,0:T(8,128)(2,1)S(1)} all-to-all(bf16[16,144,256]{2,1,0:T(8,128)(2,1)S(1)} %attend.1), channel_id=1, replica_groups=mesh['zh'=2,'x1'=2,'x0'=2,'c'=2,'y'=4,'zl1'=2,'zl0'=2] {'y','x0','zl0'}, dimensions={0} | all-to-all | bytes 2359296 | tf_op jit(solution)/shard_map/all_to_all | solution.py:184
  94.6 1.1 sum.1
  95.8 32.0 %all_to_all.21.in_ref = bf16[32,72,128]{2,1,0:T(8,128)(2,1)S(1)} all-to-all(bf16[32,72,128]{2,1,0:T(8,128)(2,1)S(1)} %bitcast.14), channel_id=1, replica_groups=mesh['zh'=2,'x1'=2,'x0'=2,'c'=2,'y'=4,'zl1'=2,'zl0'=2] {'zh','x1','x0','..., dimensions={0} | all-to-all | bytes 1179648 | tf_op jit(solution)/shard_map/all_to_all | solution.py:194
  127.8 1.2 unpack.1
  (4 shorter events, 0.0 us)
Async XLA Ops:
  0.6 43.7 %copy-start = (s32[16]{0:T(128)S(1)}, s32[16]{0:T(128)}, u32[]{:S(2)}) copy-start(s32[16]{0:T(128)} %param.11) | copy-start | bytes 196
  0.6 0.9 copy-start.1
  1.6 0.9 copy-start.2
  2.5 0.9 copy-start.3
  3.4 0.9 copy-start.4
  4.3 14.0 %copy-start.5 = (s32[16,2]{0,1:T(2,128)S(1)}, s32[16,2]{0,1:T(2,128)}, u32[]{:S(2)}) copy-start(s32[16,2]{0,1:T(2,128)} %param.10) | copy-start | bytes 388
  5.7 30.5 %all-to-all-start = ((bf16[32,72,128]{2,1,0:T(8,128)(2,1)}), bf16[32,72,128]{2,1,0:T(8,128)(2,1)S(1)}, u32[]{:S(2)}, u32[]{:S(2)}) async-start(bf16[32,72,128]{2,1,0:T(8,128)(2,1)} %pack.1), calls=%async_computation | async-start | bytes 1179648 | tf_op jit(solution)/shard_map/all_to_all | solution.py:178
  38.2 20.8 %all-to-all-start.1 = ((bf16[16,144,256]{2,1,0:T(8,128)(2,1)}), bf16[16,144,256]{2,1,0:T(8,128)(2,1)S(1)}, u32[]{:S(2)}, u32[]{:S(2)}) async-start(bf16[16,144,256]{2,1,0:T(8,128)(2,1)} %pick.1), calls=%async_computation.1 | async-start | bytes 2359296 | tf_op jit(solution)/shard_map/all_to_all | solution.py:182

commit v3 on v2

--- a/solution.py
+++ b/solution.py
@@ -9,10 +9,12 @@
 
 DH = 64
 HALF = DH // 2
+REST = 16
 HIDDEN_MOST = 288
 BF16 = jnp.bfloat16
 F32 = jnp.float32
 VMEM = pl.BlockSpec(memory_space=pltpu.VMEM)
+HBM = pl.BlockSpec(memory_space=pltpu.HBM)
 SMEM = pl.BlockSpec(memory_space=pltpu.SMEM)
 
 FINE = (("zh", 2), ("x1", 2), ("x0", 2), ("c", 2), ("y", 4), ("zl1", 2), ("zl0", 2))
@@ -28,19 +30,36 @@
     return slice(DH * head + HALF * half, DH * head + HALF * (half + 1))
 
 
-def pack_kernel(q_ref, d_ref, k_ref, v_ref, out_ref):
+def pack_kernel(q_hbm, d_hbm, k_hbm, v_hbm, out_ref, q_ref, d_ref, k_ref, v_ref, sems):
+    refs = (q_ref, d_ref, k_ref, v_ref)
+    copies = [pltpu.make_async_copy(a, b, sems.at[i]) for i, (a, b) in enumerate(zip((q_hbm, d_hbm, k_hbm, v_hbm), refs))]
+    for copy in copies:
+        copy.start()
+    for copy in copies:
+        copy.wait()
     for head in range(q_ref.shape[1] // DH):
         for half in range(2):
-            parts = [ref[:, columns(head, half)] for ref in (q_ref, d_ref, k_ref, v_ref)]
+            parts = [ref[:, columns(head, half)] for ref in refs]
             out_ref[piece(head, half)] = jnp.concatenate(parts, axis=1)
 
 
 def unpack_kernel(in_ref, q_ref, k_ref, v_ref):
+    def unfold(at):
+        x = in_ref[at].astype(F32)
+        lane = lax.broadcasted_iota(jnp.int32, (REST, 128), 1)
+        q, k, v = (pltpu.roll(x[REST * i : REST * (i + 1)], shift, 1) for i, shift in enumerate((128 - HALF, HALF, 2 * HALF)))
+        return jnp.concatenate([x, jnp.where(lane < HALF, q, jnp.where(lane < 3 * HALF, k, v))], axis=0)
+
     for pair in range(q_ref.shape[1] // (2 * DH)):
+        parts = [unfold(piece(2 * pair + i // 2, i % 2)) for i in range(4)]
+        lane = lax.broadcasted_iota(jnp.int32, parts[0].shape, 1)
         for out, place in ((q_ref, 0), (k_ref, 2), (v_ref, 3)):
-            lanes = slice(HALF * place, HALF * (place + 1))
-            parts = [in_ref[piece(2 * pair + i // 2, i % 2)][:, lanes] for i in range(4)]
-            out[:, 2 * DH * pair : 2 * DH * (pair + 1)] = jnp.concatenate(parts, axis=1)
+            row = parts[place]
+            for i in range(4):
+                if i != place:
+                    turned = pltpu.roll(parts[i], (HALF * (i - place)) % 128, 1)
+                    row = jnp.where((lane >= HALF * i) & (lane < HALF * (i + 1)), turned, row)
+            out[:, 2 * DH * pair : 2 * DH * (pair + 1)] = row.astype(BF16)
 
 
 def pick_kernel(partners_ref, in_ref, out_ref):
@@ -60,8 +79,16 @@
         one, two = partners_ref[group, 0], partners_ref[group, 1]
         total[one] += jnp.where(left, 0.0, pltpu.roll(listed, DH, 1))
         total[two] += jnp.where(left, 0.0, listed)
+    folded = out_ref.shape[1]
+    lane = lax.broadcasted_iota(jnp.int32, (folded, 128), 1)
+    spare = (lane >= HALF) & (lane < DH)
     for group in range(groups):
-        out_ref[group] = total[group].astype(BF16)
+        for chunk in range(2):
+            x = total[group, chunk * (folded + REST) : (chunk + 1) * (folded + REST)]
+            rest = x[folded:]
+            fill = [pltpu.roll(rest, shift, 1) for shift in (HALF, 128 - HALF, 128 - 2 * HALF)]
+            fill = jnp.concatenate(fill + [jnp.zeros((folded - 3 * REST, 128), F32)], axis=0)
+            out_ref[2 * group + chunk] = jnp.where(spare, fill, x[:folded]).astype(BF16)
 
 
 WIDE = 256
@@ -173,7 +200,9 @@
     pieces = 2 * width // DH
     small = pltpu.CompilerParams(vmem_limit_bytes=32 * 2**20)
     packed = pl.pallas_call(
-        pack_kernel, out_shape=shape(pieces, rows, 128), in_specs=[VMEM] * 4, out_specs=VMEM, name="pack", compiler_params=small
+        pack_kernel, out_shape=shape(pieces, rows, 128), in_specs=[HBM] * 4, out_specs=VMEM, name="pack",
+        compiler_params=pltpu.CompilerParams(vmem_limit_bytes=63_400_000),
+        scratch_shapes=[pltpu.VMEM((rows, width), BF16)] * 4 + [pltpu.SemaphoreType.DMA((4,))],
     )(queries[0], grad_out[0], keys_in[0], values_in[0])
     by_group = lax.all_to_all(packed, OUTER, 0, 0, tiled=True).reshape(groups, 2 * rows, 128)
     picked = pl.pallas_call(
@@ -184,14 +213,14 @@
     spread = lax.all_to_all(attend(hidden, gathered), INNER, 0, 0, tiled=True)
     summed = pl.pallas_call(
         sum_kernel,
-        out_shape=shape(groups, 2 * rows, 128),
+        out_shape=shape(pieces, rows - REST, 128),
         in_specs=[SMEM, VMEM],
         out_specs=VMEM,
         scratch_shapes=[pltpu.VMEM((groups, 2 * rows, 128), F32)],
         name="sum",
         compiler_params=small,
     )(partners, spread)
-    by_head = lax.all_to_all(summed.reshape(pieces, rows, 128), OUTER, 0, 0, tiled=True)
+    by_head = lax.all_to_all(summed, OUTER, 0, 0, tiled=True)
     dq, dk, dv = pl.pallas_call(
         unpack_kernel, out_shape=(shape(rows, width),) * 3, in_specs=[VMEM], out_specs=(VMEM,) * 3, name="unpack", compiler_params=small
     )(by_head)

time: 129 us -> 125 us (0.969)
  local copies, waits for them, and re-layouts: 4.56 us -> 0.92 us
  blocking collectives: 50.3 us -> 47.5 us
  Pallas kernels: 23.2 us -> 24.9 us
    unnamed x13 -> x5, local copies, waits for them, and re-layouts: 3.73 us -> 0.1 us
    all_to_all x1, blocking collectives: 32 us -> 29.2 us  [local(): by_head = lax.all_to_all(summed, OUTER, 0, 0, tiled=True)]
where the time goes in v3:
time: 125 us; the launch traced here: 124 us
  blocking collectives  47.5 us (38%)
  waiting for transfers between devices  31.9 us (26%)
  Pallas kernels  24.9 us (20%)
  starting transfers between devices  18.5 us (15%)
    all_to_all x1, blocking collectives, local(): by_head = lax.all_to_all(summed, OUTER, 0, 0, tiled=True)  29.2 us
    all_to_all x1, blocking collectives, local(): spread = lax.all_to_all(attend(hidden, gathered), INNER, 0, 0, tiled=True)  18.3 us
    all_to_all x1, waiting for transfers between devices, local(): lax.all_to_all(packed, OUTER, 0, 0, tiled=True)  17.8 us
    pallas_call x1, Pallas kernels, attend(): pl.pallas_call(attend_kernel, out_shape=shape(*rows.shape), in_specs=[SME...  17.4 us
    all_to_all x1, waiting for transfers between devices, local(): gathered = lax.all_to_all(picked, INNER, 0, 0, tiled=True)  14 us
    all_to_all x1, starting transfers between devices, local(): lax.all_to_all(packed, OUTER, 0, 0, tiled=True)  12.6 us
    all_to_all x1, starting transfers between devices, local(): gathered = lax.all_to_all(picked, INNER, 0, 0, tiled=True)  5.87 us
    pallas_call x1, Pallas kernels, local(): pl.pallas_call(pack_kernel, out_shape=shape(pieces, rows, 128), in_specs=...  2.57 us
  transfers between devices with their start and end apart: 2, of which 2 were waited for; matrix products, arithmetic and copies ran while one was open for 1% of the time, Pallas kernels for 0%

profile of v3, /device:TPU:1, one launch (start us, length us, event | category | flops | bytes accessed | tf_op | source)
XLA Modules:
  0.0 124.4 jit_solution(15524001929623448978)
XLA Ops:
  0.6 0.0 copy-start
  0.6 0.0 copy-start.1
  0.7 2.6 %pack.1 = bf16[32,72,128]{2,1,0:T(8,128)(2,1)} custom-call(bf16[72,1024]{1,0:T(8,128)(2,1)} %bitcast.13, bf16[72,1024]{1,0:T(8,128)(2,1)} %bitcast.14, bf16[72,1024]{1,0:T(8,128)(2,1)} %bitcast.15, bf16[72,1024]{1,0:T(8,128)(2,1)} %bitcast.16), custom_call_target="tpu_custom_call" | custom-call | tf_op jit(solution)/shard_map/pack/pallas_call | solution.py:202
  3.2 12.6 %all-to-all-start = ((bf16[32,72,128]{2,1,0:T(8,128)(2,1)}), bf16[32,72,128]{2,1,0:T(8,128)(2,1)S(1)}, u32[]{:S(2)}, u32[]{:S(2)}) async-start(bf16[32,72,128]{2,1,0:T(8,128)(2,1)} %pack.1), calls=%async_computation | async-start | bytes 1179648 | tf_op jit(solution)/shard_map/all_to_all | solution.py:207
  15.8 0.0 copy-done.1
  15.8 0.1 copy.12.partners_ref
  15.9 17.8 %all-to-all-done = bf16[32,72,128]{2,1,0:T(8,128)(2,1)S(1)} async-done(((bf16[32,72,128]{2,1,0:T(8,128)(2,1)}), bf16[32,72,128]{2,1,0:T(8,128)(2,1)S(1)}, u32[]{:S(2)}, u32[]{:S(2)}) %all-to-all-start) | async-done | bytes 589856 | tf_op jit(solution)/shard_map/all_to_all | solution.py:207
  33.8 2.0 %pick.1 = bf16[16,144,256]{2,1,0:T(8,128)(2,1)} custom-call(s32[16,2]{1,0:T(8,128)S(1)} %copy.12.partners_ref, bf16[16,144,128]{2,1,0:T(8,128)(2,1)S(1)} %bitcast.12), custom_call_target="tpu_custom_call" | custom-call | tf_op jit(solution)/shard_map/pick/pallas_call | solution.py:208
  35.7 5.9 %all-to-all-start.1 = ((bf16[16,144,256]{2,1,0:T(8,128)(2,1)}), bf16[16,144,256]{2,1,0:T(8,128)(2,1)S(1)}, u32[]{:S(2)}, u32[]{:S(2)}) async-start(bf16[16,144,256]{2,1,0:T(8,128)(2,1)} %pick.1), calls=%async_computation.1 | async-start | bytes 2359296 | tf_op jit(solution)/shard_map/all_to_all | solution.py:211
  41.6 0.2 dynamic-slice_reduce_fusion
  41.8 0.0 copy-done
  41.8 0.6 gather_fusion
  42.5 14.0 %all-to-all-done.1.in_ref = bf16[16,144,256]{2,1,0:T(8,128)(2,1)S(1)} async-done(((bf16[16,144,256]{2,1,0:T(8,128)(2,1)}), bf16[16,144,256]{2,1,0:T(8,128)(2,1)S(1)}, u32[]{:S(2)}, u32[]{:S(2)}) %all-to-all-start.1) | async-done | bytes 1179680 | tf_op jit(solution)/shard_map/all_to_all | solution.py:211
  56.5 17.4 %attend.1 = bf16[16,144,256]{2,1,0:T(8,128)(2,1)S(1)} custom-call(s32[2]{0:T(128)S(1)} %gather_fusion, bf16[16,144,256]{2,1,0:T(8,128)(2,1)S(1)} %all-to-all-done.1.in_ref), custom_call_target="tpu_custom_call" | custom-call | tf_op jit(solution)/shard_map/attend/pallas_call | solution.py:178
  73.9 18.3 %all_to_all.20.in_ref = bf16[16,144,256]{2,1,0:T(8,128)(2,1)S(1)} all-to-all(bf16[16,144,256]{2,1,0:T(8,128)(2,1)S(1)} %attend.1), channel_id=1, replica_groups=mesh['zh'=2,'x1'=2,'x0'=2,'c'=2,'y'=4,'zl1'=2,'zl0'=2] {'y','x0','zl0'}, dimensions={0} | all-to-all | bytes 2359296 | tf_op jit(solution)/shard_map/all_to_all | solution.py:213
  92.2 1.3 %sum.1 = bf16[32,56,128]{2,1,0:T(8,128)(2,1)S(1)} custom-call(s32[16,2]{1,0:T(8,128)S(1)} %copy.12.partners_ref, bf16[16,144,256]{2,1,0:T(8,128)(2,1)S(1)} %all_to_all.20.in_ref), custom_call_target="tpu_custom_call" | custom-call | tf_op jit(solution)/shard_map/sum/pallas_call | solution.py:214
  93.5 29.2 %all_to_all.21.in_ref = bf16[32,56,128]{2,1,0:T(8,128)(2,1)S(1)} all-to-all(bf16[32,56,128]{2,1,0:T(8,128)(2,1)S(1)} %sum.1), channel_id=1, replica_groups=mesh['zh'=2,'x1'=2,'x0'=2,'c'=2,'y'=4,'zl1'=2,'zl0'=2] {'zh','x1','x0','..., dimensions={0} | all-to-all | bytes 917504 | tf_op jit(solution)/shard_map/all_to_all | solution.py:223
  122.7 1.6 %unpack.1 = (bf16[72,1024]{1,0:T(8,128)(2,1)}, bf16[72,1024]{1,0:T(8,128)(2,1)}, bf16[72,1024]{1,0:T(8,128)(2,1)}) custom-call(bf16[32,56,128]{2,1,0:T(8,128)(2,1)S(1)} %all_to_all.21.in_ref), custom_call_target="tpu_custom_call" | custom-call | tf_op jit(solution)/shard_map/unpack/pallas_call | solution.py:224
  (2 shorter events, 0.0 us)
Async XLA Ops:
  0.6 41.2 %copy-start = (s32[16]{0:T(128)S(1)}, s32[16]{0:T(128)}, u32[]{:S(2)}) copy-start(s32[16]{0:T(128)} %param.11) | copy-start | bytes 196
  0.6 15.2 %copy-start.1 = (s32[16,2]{0,1:T(2,128)S(1)}, s32[16,2]{0,1:T(2,128)}, u32[]{:S(2)}) copy-start(s32[16,2]{0,1:T(2,128)} %param.10) | copy-start | bytes 388
  3.2 30.5 %all-to-all-start = ((bf16[32,72,128]{2,1,0:T(8,128)(2,1)}), bf16[32,72,128]{2,1,0:T(8,128)(2,1)S(1)}, u32[]{:S(2)}, u32[]{:S(2)}) async-start(bf16[32,72,128]{2,1,0:T(8,128)(2,1)} %pack.1), calls=%async_computation | async-start | bytes 1179648 | tf_op jit(solution)/shard_map/all_to_all | solution.py:207
  35.7 20.8 %all-to-all-start.1 = ((bf16[16,144,256]{2,1,0:T(8,128)(2,1)}), bf16[16,144,256]{2,1,0:T(8,128)(2,1)S(1)}, u32[]{:S(2)}, u32[]{:S(2)}) async-start(bf16[16,144,256]{2,1,0:T(8,128)(2,1)} %pick.1), calls=%async_computation.1 | async-start | bytes 2359296 | tf_op jit(solution)/shard_map/all_to_all | solution.py:211

commit v4 on v3

--- a/solution.py
+++ b/solution.py
@@ -91,10 +91,10 @@
             out_ref[2 * group + chunk] = jnp.where(spare, fill, x[:folded]).astype(BF16)
 
 
-WIDE = 256
-
-
-def attend_kernel(hidden_ref, in_ref, out_ref, own, listed, kt, bias, s_ref, dp_ref, total):
+WIDE = 1152
+
+
+def attend_kernel(hidden_ref, in_ref, out_ref, own, listed, kt, bias, s_ref, dp_ref, total, flat, dqt):
     sources, rows_of = in_ref.shape[:2]
     seq = own.shape[0]
     blocks = [(s // 4 * 2 + s % 2, s // 2 % 2) for s in range(sources)]
@@ -103,9 +103,12 @@
         lanes = slice(128 * half, 128 * (half + 1))
         own[rows, lanes] = in_ref[source, :, 0:128]
         listed[rows, lanes] = in_ref[source, :, 128:256]
-    for j, (keys, place) in enumerate(((own, DH), (listed, 0), (listed, DH))):
-        both = keys[...].T
-        kt[j] = jnp.concatenate([both[place : place + HALF], both[128 + place : 128 + place + HALF]], axis=0)
+    flipped = (own[...].T, listed[...].T)
+    both = lambda x, place: jnp.concatenate([x[place : place + HALF], x[128 + place : 128 + place + HALF]], axis=0)
+    for j, (x, place) in enumerate(((flipped[0], DH), (flipped[1], 0), (flipped[1], DH))):
+        kt[j] = both(x, place)
+    flat[:DH] = (both(flipped[0], 0).astype(F32) * 0.125).astype(BF16)
+    flat[DH:] = both(flipped[0], HALF)
     index = lax.broadcasted_iota(jnp.int32, bias.shape[1:], 0)
     chunk = rows_of // 2
     swap = (index >= chunk) & (index < 3 * chunk)
@@ -148,13 +151,10 @@
         for j, (_, q_side, d_side) in enumerate(terms):
             prob = s_ref[j, :, :size] * inv
             dscore = (prob * (dp_ref[j, :, :size] - delta)).astype(BF16)
-            both = jnp.concatenate([dscore, prob.astype(BF16)], axis=1)
-            sides = jnp.concatenate([q_side, d_side], axis=0)
-            total[min(j, 1)] += jnp.dot(both, sides, preferred_element_type=F32)
+            total[j, :DH] += lax.dot_general(flat[:DH, rows], dscore, nt, preferred_element_type=F32)
+            total[j, DH:] += lax.dot_general(flat[DH:, rows], prob.astype(BF16), nt, preferred_element_type=F32)
             dq += jnp.dot(kt[j], dscore, preferred_element_type=F32)
-        dq = dq * 0.125
-        gap = jnp.zeros((128 - HALF, size), F32)
-        total[0, rows, :] += jnp.concatenate([dq[:HALF], gap, dq[HALF:], gap], axis=0).T
+        dqt[:, rows] = dq
 
     @pl.loop(0, seq // WIDE)
     def _(i):
@@ -162,11 +162,17 @@
 
     if seq % WIDE:
         tile(seq // WIDE * WIDE, seq % WIDE)
-    for source, (block, half) in enumerate(blocks):
-        rows = slice(block * rows_of, (block + 1) * rows_of)
-        lanes = slice(128 * half, 128 * (half + 1))
-        out_ref[source, :, 0:128] = total[0, rows, lanes].astype(BF16)
-        out_ref[source, :, 128:256] = total[1, rows, lanes].astype(BF16)
+    gap = jnp.zeros((HALF, seq), F32)
+    for half in range(2):
+        part = slice(HALF * half, HALF * (half + 1))
+        value = slice(DH + HALF * half, DH + HALF * (half + 1))
+        own_part = jnp.concatenate([dqt[part] * 0.125, gap, total[0, part], total[0, value]], axis=0).T.astype(BF16)
+        listed_part = jnp.concatenate([total[1, part], total[1, value], total[2, part], total[2, value]], axis=0).T.astype(BF16)
+        for source, (block, which) in enumerate(blocks):
+            if which == half:
+                rows = slice(block * rows_of, (block + 1) * rows_of)
+                out_ref[source, :, 0:128] = own_part[rows]
+                out_ref[source, :, 128:256] = listed_part[rows]
 
 
 def shape(*dims):
@@ -187,9 +193,11 @@
             pltpu.VMEM((2, HIDDEN_MOST, WIDE), F32),
             pltpu.VMEM((3, seq, WIDE), F32),
             pltpu.VMEM((3, seq, WIDE), F32),
-            pltpu.VMEM((2, seq, 256), F32),
+            pltpu.VMEM((3, 2 * DH, seq), F32),
+            pltpu.VMEM((2 * DH, seq), BF16),
+            pltpu.VMEM((DH, seq), F32),
         ],
-        compiler_params=pltpu.CompilerParams(vmem_limit_bytes=48 * 2**20),
+        compiler_params=pltpu.CompilerParams(vmem_limit_bytes=46 * 2**20),
         name="attend",
     )(hidden, rows)
 

time: 125 us -> 122 us (0.976)
  Pallas kernels: 24.9 us -> 22.6 us
    pallas_call x1, Pallas kernels: 17.4 us -> 15.2 us  [attend(): pl.pallas_call(attend_kernel, out_shape=shape(*rows.shape), in_specs=[SME...]
where the time goes in v4:
time: 122 us
  blocking collectives  47.5 us (39%)
  waiting for transfers between devices  31.9 us (26%)
  Pallas kernels  22.6 us (19%)
  starting transfers between devices  18.5 us (15%)
    all_to_all x1, blocking collectives, local(): by_head = lax.all_to_all(summed, OUTER, 0, 0, tiled=True)  29.3 us
    all_to_all x1, blocking collectives, local(): spread = lax.all_to_all(attend(hidden, gathered), INNER, 0, 0, tiled=True)  18.2 us
    all_to_all x1, waiting for transfers between devices, local(): lax.all_to_all(packed, OUTER, 0, 0, tiled=True)  17.8 us
    pallas_call x1, Pallas kernels, attend(): pl.pallas_call(attend_kernel, out_shape=shape(*rows.shape), in_specs=[SME...  15.2 us
    all_to_all x1, waiting for transfers between devices, local(): gathered = lax.all_to_all(picked, INNER, 0, 0, tiled=True)  14 us
    all_to_all x1, starting transfers between devices, local(): lax.all_to_all(packed, OUTER, 0, 0, tiled=True)  12.6 us
    all_to_all x1, starting transfers between devices, local(): gathered = lax.all_to_all(picked, INNER, 0, 0, tiled=True)  5.87 us
    pallas_call x1, Pallas kernels, local(): pl.pallas_call(pack_kernel, out_shape=shape(pieces, rows, 128), in_specs=...  2.57 us
  transfers between devices with their start and end apart: 2, of which 2 were waited for; matrix products, arithmetic and copies ran while one was open for 1% of the time, Pallas kernels for 0%

profile of v4, /device:TPU:1, one launch (start us, length us, event | category | flops | bytes accessed | tf_op | source)
XLA Modules:
  0.0 122.1 jit_solution(11134416083077186534)
XLA Ops:
  0.6 0.0 copy-start
  0.6 0.0 copy-start.1
  0.7 2.6 %pack.1 = bf16[32,72,128]{2,1,0:T(8,128)(2,1)} custom-call(bf16[72,1024]{1,0:T(8,128)(2,1)} %bitcast.13, bf16[72,1024]{1,0:T(8,128)(2,1)} %bitcast.14, bf16[72,1024]{1,0:T(8,128)(2,1)} %bitcast.15, bf16[72,1024]{1,0:T(8,128)(2,1)} %bitcast.16), custom_call_target="tpu_custom_call" | custom-call | tf_op jit(solution)/shard_map/pack/pallas_call | solution.py:210
  3.2 12.6 %all-to-all-start = ((bf16[32,72,128]{2,1,0:T(8,128)(2,1)}), bf16[32,72,128]{2,1,0:T(8,128)(2,1)S(1)}, u32[]{:S(2)}, u32[]{:S(2)}) async-start(bf16[32,72,128]{2,1,0:T(8,128)(2,1)} %pack.1), calls=%async_computation | async-start | bytes 1179648 | tf_op jit(solution)/shard_map/all_to_all | solution.py:215
  15.8 0.0 copy-done.1
  15.8 0.1 copy.12.partners_ref
  15.9 17.8 %all-to-all-done = bf16[32,72,128]{2,1,0:T(8,128)(2,1)S(1)} async-done(((bf16[32,72,128]{2,1,0:T(8,128)(2,1)}), bf16[32,72,128]{2,1,0:T(8,128)(2,1)S(1)}, u32[]{:S(2)}, u32[]{:S(2)}) %all-to-all-start) | async-done | bytes 589856 | tf_op jit(solution)/shard_map/all_to_all | solution.py:215
  33.8 2.0 %pick.1 = bf16[16,144,256]{2,1,0:T(8,128)(2,1)} custom-call(s32[16,2]{1,0:T(8,128)S(1)} %copy.12.partners_ref, bf16[16,144,128]{2,1,0:T(8,128)(2,1)S(1)} %bitcast.12), custom_call_target="tpu_custom_call" | custom-call | tf_op jit(solution)/shard_map/pick/pallas_call | solution.py:216
  35.7 5.9 %all-to-all-start.1 = ((bf16[16,144,256]{2,1,0:T(8,128)(2,1)}), bf16[16,144,256]{2,1,0:T(8,128)(2,1)S(1)}, u32[]{:S(2)}, u32[]{:S(2)}) async-start(bf16[16,144,256]{2,1,0:T(8,128)(2,1)} %pick.1), calls=%async_computation.1 | async-start | bytes 2359296 | tf_op jit(solution)/shard_map/all_to_all | solution.py:219
  41.6 0.2 dynamic-slice_reduce_fusion
  41.8 0.0 copy-done
  41.8 0.6 gather_fusion
  42.5 14.0 %all-to-all-done.1.in_ref = bf16[16,144,256]{2,1,0:T(8,128)(2,1)S(1)} async-done(((bf16[16,144,256]{2,1,0:T(8,128)(2,1)}), bf16[16,144,256]{2,1,0:T(8,128)(2,1)S(1)}, u32[]{:S(2)}, u32[]{:S(2)}) %all-to-all-start.1) | async-done | bytes 1179680 | tf_op jit(solution)/shard_map/all_to_all | solution.py:219
  56.5 15.2 %attend.1 = bf16[16,144,256]{2,1,0:T(8,128)(2,1)S(1)} custom-call(s32[2]{0:T(128)S(1)} %gather_fusion, bf16[16,144,256]{2,1,0:T(8,128)(2,1)S(1)} %all-to-all-done.1.in_ref), custom_call_target="tpu_custom_call" | custom-call | tf_op jit(solution)/shard_map/attend/pallas_call | solution.py:184
  71.7 18.2 %all_to_all.20.in_ref = bf16[16,144,256]{2,1,0:T(8,128)(2,1)S(1)} all-to-all(bf16[16,144,256]{2,1,0:T(8,128)(2,1)S(1)} %attend.1), channel_id=1, replica_groups=mesh['zh'=2,'x1'=2,'x0'=2,'c'=2,'y'=4,'zl1'=2,'zl0'=2] {'y','x0','zl0'}, dimensions={0} | all-to-all | bytes 2359296 | tf_op jit(solution)/shard_map/all_to_all | solution.py:221
  89.9 1.3 %sum.1 = bf16[32,56,128]{2,1,0:T(8,128)(2,1)S(1)} custom-call(s32[16,2]{1,0:T(8,128)S(1)} %copy.12.partners_ref, bf16[16,144,256]{2,1,0:T(8,128)(2,1)S(1)} %all_to_all.20.in_ref), custom_call_target="tpu_custom_call" | custom-call | tf_op jit(solution)/shard_map/sum/pallas_call | solution.py:222
  91.2 29.3 %all_to_all.21.in_ref = bf16[32,56,128]{2,1,0:T(8,128)(2,1)S(1)} all-to-all(bf16[32,56,128]{2,1,0:T(8,128)(2,1)S(1)} %sum.1), channel_id=1, replica_groups=mesh['zh'=2,'x1'=2,'x0'=2,'c'=2,'y'=4,'zl1'=2,'zl0'=2] {'zh','x1','x0','..., dimensions={0} | all-to-all | bytes 917504 | tf_op jit(solution)/shard_map/all_to_all | solution.py:231
  120.5 1.6 %unpack.1 = (bf16[72,1024]{1,0:T(8,128)(2,1)}, bf16[72,1024]{1,0:T(8,128)(2,1)}, bf16[72,1024]{1,0:T(8,128)(2,1)}) custom-call(bf16[32,56,128]{2,1,0:T(8,128)(2,1)S(1)} %all_to_all.21.in_ref), custom_call_target="tpu_custom_call" | custom-call | tf_op jit(solution)/shard_map/unpack/pallas_call | solution.py:232
  (2 shorter events, 0.0 us)
Async XLA Ops:
  0.6 41.2 %copy-start = (s32[16]{0:T(128)S(1)}, s32[16]{0:T(128)}, u32[]{:S(2)}) copy-start(s32[16]{0:T(128)} %param.11) | copy-start | bytes 196
  0.6 15.2 %copy-start.1 = (s32[16,2]{0,1:T(2,128)S(1)}, s32[16,2]{0,1:T(2,128)}, u32[]{:S(2)}) copy-start(s32[16,2]{0,1:T(2,128)} %param.10) | copy-start | bytes 388
  3.2 30.5 %all-to-all-start = ((bf16[32,72,128]{2,1,0:T(8,128)(2,1)}), bf16[32,72,128]{2,1,0:T(8,128)(2,1)S(1)}, u32[]{:S(2)}, u32[]{:S(2)}) async-start(bf16[32,72,128]{2,1,0:T(8,128)(2,1)} %pack.1), calls=%async_computation | async-start | bytes 1179648 | tf_op jit(solution)/shard_map/all_to_all | solution.py:215
  35.7 20.8 %all-to-all-start.1 = ((bf16[16,144,256]{2,1,0:T(8,128)(2,1)}), bf16[16,144,256]{2,1,0:T(8,128)(2,1)S(1)}, u32[]{:S(2)}, u32[]{:S(2)}) async-start(bf16[16,144,256]{2,1,0:T(8,128)(2,1)} %pick.1), calls=%async_computation.1 | async-start | bytes 2359296 | tf_op jit(solution)/shard_map/all_to_all | solution.py:219

commit v5 on v4

--- a/solution.py
+++ b/solution.py
@@ -28,6 +28,28 @@
 
 def columns(head, half):
     return slice(DH * head + HALF * half, DH * head + HALF * (half + 1))
+
+
+def slots(rows):
+    return lax.broadcasted_iota(jnp.int32, (rows, 128), 1) // HALF
+
+
+def spare(rows):
+    return slots(rows) == 1
+
+
+def to_spare(x, slot):
+    return x if slot == 1 else pltpu.roll(x, (HALF - HALF * slot) % 128, 1)
+
+
+def from_spare(x, start, places):
+    slot = slots(REST)
+    out = jnp.zeros((REST, 128), F32)
+    for i, place in enumerate(places):
+        part = x[start + REST * i : start + REST * (i + 1)]
+        part = part if place == 1 else pltpu.roll(part, (HALF * place - HALF) % 128, 1)
+        out = jnp.where(slot == place, part, out)
+    return out
 
 
 def pack_kernel(q_hbm, d_hbm, k_hbm, v_hbm, out_ref, q_ref, d_ref, k_ref, v_ref, sems):
@@ -46,9 +68,7 @@
 def unpack_kernel(in_ref, q_ref, k_ref, v_ref):
     def unfold(at):
         x = in_ref[at].astype(F32)
-        lane = lax.broadcasted_iota(jnp.int32, (REST, 128), 1)
-        q, k, v = (pltpu.roll(x[REST * i : REST * (i + 1)], shift, 1) for i, shift in enumerate((128 - HALF, HALF, 2 * HALF)))
-        return jnp.concatenate([x, jnp.where(lane < HALF, q, jnp.where(lane < 3 * HALF, k, v))], axis=0)
+        return jnp.concatenate([x, from_spare(x, 0, (0, 2, 3))], axis=0)
 
     for pair in range(q_ref.shape[1] // (2 * DH)):
         parts = [unfold(piece(2 * pair + i // 2, i % 2)) for i in range(4)]
@@ -70,25 +90,26 @@
 
 
 def sum_kernel(partners_ref, in_ref, out_ref, total):
-    groups = in_ref.shape[0]
+    groups, sent = in_ref.shape[:2]
     for group in range(groups):
-        total[group] = in_ref[group, :, 0:128].astype(F32)
-    left = lax.broadcasted_iota(jnp.int32, total.shape[1:], 1) < DH
+        x = in_ref[group, :, 0:128].astype(F32)
+        total[group, :sent] = x
+        total[group, sent:] = from_spare(x, 0, (0, 2, 3))
+    left = slots(sent + REST) < 2
     for group in range(groups):
         listed = in_ref[group, :, 128:256].astype(F32)
+        rest = from_spare(in_ref[group, :, 0:128].astype(F32), 3 * REST, range(4))
+        listed = jnp.concatenate([listed, rest], axis=0)
         one, two = partners_ref[group, 0], partners_ref[group, 1]
         total[one] += jnp.where(left, 0.0, pltpu.roll(listed, DH, 1))
         total[two] += jnp.where(left, 0.0, listed)
     folded = out_ref.shape[1]
-    lane = lax.broadcasted_iota(jnp.int32, (folded, 128), 1)
-    spare = (lane >= HALF) & (lane < DH)
     for group in range(groups):
         for chunk in range(2):
             x = total[group, chunk * (folded + REST) : (chunk + 1) * (folded + REST)]
-            rest = x[folded:]
-            fill = [pltpu.roll(rest, shift, 1) for shift in (HALF, 128 - HALF, 128 - 2 * HALF)]
+            fill = [to_spare(x[folded:], slot) for slot in (0, 2, 3)]
             fill = jnp.concatenate(fill + [jnp.zeros((folded - 3 * REST, 128), F32)], axis=0)
-            out_ref[2 * group + chunk] = jnp.where(spare, fill, x[:folded]).astype(BF16)
+            out_ref[2 * group + chunk] = jnp.where(spare(folded), fill, x[:folded]).astype(BF16)
 
 
 WIDE = 1152
@@ -163,16 +184,20 @@
     if seq % WIDE:
         tile(seq // WIDE * WIDE, seq % WIDE)
     gap = jnp.zeros((HALF, seq), F32)
+    folded = out_ref.shape[1]
     for half in range(2):
         part = slice(HALF * half, HALF * (half + 1))
         value = slice(DH + HALF * half, DH + HALF * (half + 1))
-        own_part = jnp.concatenate([dqt[part] * 0.125, gap, total[0, part], total[0, value]], axis=0).T.astype(BF16)
-        listed_part = jnp.concatenate([total[1, part], total[1, value], total[2, part], total[2, value]], axis=0).T.astype(BF16)
+        own_part = jnp.concatenate([dqt[part] * 0.125, gap, total[0, part], total[0, value]], axis=0).T
+        listed_part = jnp.concatenate([total[1, part], total[1, value], total[2, part], total[2, value]], axis=0).T
         for source, (block, which) in enumerate(blocks):
             if which == half:
-                rows = slice(block * rows_of, (block + 1) * rows_of)
-                out_ref[source, :, 0:128] = own_part[rows]
-                out_ref[source, :, 128:256] = listed_part[rows]
+                rows = slice(block * rows_of, block * rows_of + folded)
+                rest = slice(block * rows_of + folded, (block + 1) * rows_of)
+                fill = [to_spare(own_part[rest], slot) for slot in (0, 2, 3)] + [to_spare(listed_part[rest], slot) for slot in range(4)]
+                fill = jnp.concatenate(fill + [jnp.zeros((folded - 7 * REST, 128), F32)], axis=0)
+                out_ref[source, :, 0:128] = jnp.where(spare(folded), fill, own_part[rows]).astype(BF16)
+                out_ref[source, :, 128:256] = listed_part[rows].astype(BF16)
 
 
 def shape(*dims):
@@ -183,7 +208,7 @@
     seq = rows.shape[0] * rows.shape[1] // 2
     return pl.pallas_call(
         attend_kernel,
-        out_shape=shape(*rows.shape),
+        out_shape=shape(rows.shape[0], rows.shape[1] - REST, 256),
         in_specs=[SMEM, VMEM],
         out_specs=VMEM,
         scratch_shapes=[

time: 122 us -> 121 us (level); the launches traced: 122 us -> 119 us
  blocking collectives: 47.5 us -> 43.4 us
  Pallas kernels: 22.6 us -> 24 us
    all_to_all x1, blocking collectives: 18.2 us -> 15.4 us  [local(): spread = lax.all_to_all(attend(hidden, gathered), INNER, 0, 0, tiled=True)]
    all_to_all x1, blocking collectives: 29.3 us -> 28 us  [local(): by_head = lax.all_to_all(summed, OUTER, 0, 0, tiled=True)]
where the time goes in v5:
time: 121 us; the launch traced here: 119 us
  blocking collectives  43.4 us (36%)
  waiting for transfers between devices  31.9 us (26%)
  Pallas kernels  24 us (20%)
  starting transfers between devices  18.5 us (15%)
    all_to_all x1, blocking collectives, local(): by_head = lax.all_to_all(summed, OUTER, 0, 0, tiled=True)  28 us
    all_to_all x1, waiting for transfers between devices, local(): lax.all_to_all(packed, OUTER, 0, 0, tiled=True)  17.8 us
    pallas_call x1, Pallas kernels, attend(): pl.pallas_call(attend_kernel, out_shape=shape(rows.shape[0], rows.shape[1...  15.7 us
    all_to_all x1, blocking collectives, local(): spread = lax.all_to_all(attend(hidden, gathered), INNER, 0, 0, tiled=True)  15.4 us
    all_to_all x1, waiting for transfers between devices, local(): gathered = lax.all_to_all(picked, INNER, 0, 0, tiled=True)  14 us
    all_to_all x1, starting transfers between devices, local(): lax.all_to_all(packed, OUTER, 0, 0, tiled=True)  12.6 us
    all_to_all x1, starting transfers between devices, local(): gathered = lax.all_to_all(picked, INNER, 0, 0, tiled=True)  5.87 us
    pallas_call x1, Pallas kernels, local(): pl.pallas_call(pack_kernel, out_shape=shape(pieces, rows, 128), in_specs=...  2.57 us
  transfers between devices with their start and end apart: 2, of which 2 were waited for; matrix products, arithmetic and copies ran while one was open for 1% of the time, Pallas kernels for 0%

profile of v5, /device:TPU:1, one launch (start us, length us, event | category | flops | bytes accessed | tf_op | source)
XLA Modules:
  0.0 119.4 jit_solution(7796455961891677354)
XLA Ops:
  0.6 0.0 copy-start
  0.6 0.0 copy-start.1
  0.7 2.6 %pack.1 = bf16[32,72,128]{2,1,0:T(8,128)(2,1)} custom-call(bf16[72,1024]{1,0:T(8,128)(2,1)} %bitcast.13, bf16[72,1024]{1,0:T(8,128)(2,1)} %bitcast.14, bf16[72,1024]{1,0:T(8,128)(2,1)} %bitcast.15, bf16[72,1024]{1,0:T(8,128)(2,1)} %bitcast.16), custom_call_target="tpu_custom_call" | custom-call | tf_op jit(solution)/shard_map/pack/pallas_call | solution.py:235
  3.2 12.6 %all-to-all-start = ((bf16[32,72,128]{2,1,0:T(8,128)(2,1)}), bf16[32,72,128]{2,1,0:T(8,128)(2,1)S(1)}, u32[]{:S(2)}, u32[]{:S(2)}) async-start(bf16[32,72,128]{2,1,0:T(8,128)(2,1)} %pack.1), calls=%async_computation | async-start | bytes 1179648 | tf_op jit(solution)/shard_map/all_to_all | solution.py:240
  15.8 0.0 copy-done.1
  15.8 0.1 copy.12.partners_ref
  15.9 17.8 %all-to-all-done = bf16[32,72,128]{2,1,0:T(8,128)(2,1)S(1)} async-done(((bf16[32,72,128]{2,1,0:T(8,128)(2,1)}), bf16[32,72,128]{2,1,0:T(8,128)(2,1)S(1)}, u32[]{:S(2)}, u32[]{:S(2)}) %all-to-all-start) | async-done | bytes 589856 | tf_op jit(solution)/shard_map/all_to_all | solution.py:240
  33.8 2.0 %pick.1 = bf16[16,144,256]{2,1,0:T(8,128)(2,1)} custom-call(s32[16,2]{1,0:T(8,128)S(1)} %copy.12.partners_ref, bf16[16,144,128]{2,1,0:T(8,128)(2,1)S(1)} %bitcast.12), custom_call_target="tpu_custom_call" | custom-call | tf_op jit(solution)/shard_map/pick/pallas_call | solution.py:241
  35.7 5.9 %all-to-all-start.1 = ((bf16[16,144,256]{2,1,0:T(8,128)(2,1)}), bf16[16,144,256]{2,1,0:T(8,128)(2,1)S(1)}, u32[]{:S(2)}, u32[]{:S(2)}) async-start(bf16[16,144,256]{2,1,0:T(8,128)(2,1)} %pick.1), calls=%async_computation.1 | async-start | bytes 2359296 | tf_op jit(solution)/shard_map/all_to_all | solution.py:244
  41.6 0.2 dynamic-slice_reduce_fusion
  41.8 0.0 copy-done
  41.8 0.6 gather_fusion
  42.5 14.0 %all-to-all-done.1.in_ref = bf16[16,144,256]{2,1,0:T(8,128)(2,1)S(1)} async-done(((bf16[16,144,256]{2,1,0:T(8,128)(2,1)}), bf16[16,144,256]{2,1,0:T(8,128)(2,1)S(1)}, u32[]{:S(2)}, u32[]{:S(2)}) %all-to-all-start.1) | async-done | bytes 1179680 | tf_op jit(solution)/shard_map/all_to_all | solution.py:244
  56.5 15.7 %attend.1 = bf16[16,128,256]{2,1,0:T(8,128)(2,1)S(1)} custom-call(s32[2]{0:T(128)S(1)} %gather_fusion, bf16[16,144,256]{2,1,0:T(8,128)(2,1)S(1)} %all-to-all-done.1.in_ref), custom_call_target="tpu_custom_call" | custom-call | tf_op jit(solution)/shard_map/attend/pallas_call | solution.py:209
  72.2 15.4 %all_to_all.20.in_ref = bf16[16,128,256]{2,1,0:T(8,128)(2,1)S(1)} all-to-all(bf16[16,128,256]{2,1,0:T(8,128)(2,1)S(1)} %attend.1), channel_id=1, replica_groups=mesh['zh'=2,'x1'=2,'x0'=2,'c'=2,'y'=4,'zl1'=2,'zl0'=2] {'y','x0','zl0'}, dimensions={0} | all-to-all | bytes 2097152 | tf_op jit(solution)/shard_map/all_to_all | solution.py:246
  87.6 2.1 %sum.1 = bf16[32,56,128]{2,1,0:T(8,128)(2,1)S(1)} custom-call(s32[16,2]{1,0:T(8,128)S(1)} %copy.12.partners_ref, bf16[16,128,256]{2,1,0:T(8,128)(2,1)S(1)} %all_to_all.20.in_ref), custom_call_target="tpu_custom_call" | custom-call | tf_op jit(solution)/shard_map/sum/pallas_call | solution.py:247
  89.7 28.0 %all_to_all.21.in_ref = bf16[32,56,128]{2,1,0:T(8,128)(2,1)S(1)} all-to-all(bf16[32,56,128]{2,1,0:T(8,128)(2,1)S(1)} %sum.1), channel_id=1, replica_groups=mesh['zh'=2,'x1'=2,'x0'=2,'c'=2,'y'=4,'zl1'=2,'zl0'=2] {'zh','x1','x0','..., dimensions={0} | all-to-all | bytes 917504 | tf_op jit(solution)/shard_map/all_to_all | solution.py:256
  117.7 1.6 %unpack.1 = (bf16[72,1024]{1,0:T(8,128)(2,1)}, bf16[72,1024]{1,0:T(8,128)(2,1)}, bf16[72,1024]{1,0:T(8,128)(2,1)}) custom-call(bf16[32,56,128]{2,1,0:T(8,128)(2,1)S(1)} %all_to_all.21.in_ref), custom_call_target="tpu_custom_call" | custom-call | tf_op jit(solution)/shard_map/unpack/pallas_call | solution.py:257
  (2 shorter events, 0.0 us)
Async XLA Ops:
  0.6 41.2 %copy-start = (s32[16]{0:T(128)S(1)}, s32[16]{0:T(128)}, u32[]{:S(2)}) copy-start(s32[16]{0:T(128)} %param.11) | copy-start | bytes 196
  0.6 15.2 %copy-start.1 = (s32[16,2]{0,1:T(2,128)S(1)}, s32[16,2]{0,1:T(2,128)}, u32[]{:S(2)}) copy-start(s32[16,2]{0,1:T(2,128)} %param.10) | copy-start | bytes 388
  3.2 30.5 %all-to-all-start = ((bf16[32,72,128]{2,1,0:T(8,128)(2,1)}), bf16[32,72,128]{2,1,0:T(8,128)(2,1)S(1)}, u32[]{:S(2)}, u32[]{:S(2)}) async-start(bf16[32,72,128]{2,1,0:T(8,128)(2,1)} %pack.1), calls=%async_computation | async-start | bytes 1179648 | tf_op jit(solution)/shard_map/all_to_all | solution.py:240
  35.7 20.8 %all-to-all-start.1 = ((bf16[16,144,256]{2,1,0:T(8,128)(2,1)}), bf16[16,144,256]{2,1,0:T(8,128)(2,1)S(1)}, u32[]{:S(2)}, u32[]{:S(2)}) async-start(bf16[16,144,256]{2,1,0:T(8,128)(2,1)} %pick.1), calls=%async_computation.1 | async-start | bytes 2359296 | tf_op jit(solution)/shard_map/all_to_all | solution.py:244

commit v6 on v5

--- a/solution.py
+++ b/solution.py
@@ -52,17 +52,28 @@
     return out
 
 
-def pack_kernel(q_hbm, d_hbm, k_hbm, v_hbm, out_ref, q_ref, d_ref, k_ref, v_ref, sems):
+def pack_kernel(q_hbm, d_hbm, k_hbm, v_hbm, out_hbm, q_ref, d_ref, k_ref, v_ref, out_ref, in_sems, out_sems):
     refs = (q_ref, d_ref, k_ref, v_ref)
-    copies = [pltpu.make_async_copy(a, b, sems.at[i]) for i, (a, b) in enumerate(zip((q_hbm, d_hbm, k_hbm, v_hbm), refs))]
-    for copy in copies:
-        copy.start()
-    for copy in copies:
+    quads = q_ref.shape[1] // (4 * DH)
+    fetched = []
+    for quad in range(quads):
+        cols = slice(4 * DH * quad, 4 * DH * (quad + 1))
+        for i, (far, near) in enumerate(zip((q_hbm, d_hbm, k_hbm, v_hbm), refs)):
+            fetched.append(pltpu.make_async_copy(far.at[:, cols], near.at[:, cols], in_sems.at[quad, i]))
+            fetched[-1].start()
+    sent = []
+    for quad in range(quads):
+        for copy in fetched[4 * quad : 4 * quad + 4]:
+            copy.wait()
+        for head in range(4 * quad, 4 * quad + 4):
+            for half in range(2):
+                parts = [ref[:, columns(head, half)] for ref in refs]
+                out_ref[piece(head, half)] = jnp.concatenate(parts, axis=1)
+        pieces = slice(8 * quad, 8 * quad + 8)
+        sent.append(pltpu.make_async_copy(out_ref.at[pieces], out_hbm.at[pieces], out_sems.at[quad]))
+        sent[-1].start()
+    for copy in sent:
         copy.wait()
-    for head in range(q_ref.shape[1] // DH):
-        for half in range(2):
-            parts = [ref[:, columns(head, half)] for ref in refs]
-            out_ref[piece(head, half)] = jnp.concatenate(parts, axis=1)
 
 
 def unpack_kernel(in_ref, q_ref, k_ref, v_ref):
@@ -82,31 +93,38 @@
             out[:, 2 * DH * pair : 2 * DH * (pair + 1)] = row.astype(BF16)
 
 
-def pick_kernel(partners_ref, in_ref, out_ref):
+def pick_kernel(partners_ref, in_ref, out_hbm, out_ref, sems):
+    sent = []
     for group in range(in_ref.shape[0]):
         out_ref[group, :, 0:128] = in_ref[group]
         one, two = in_ref[partners_ref[group, 0]], in_ref[partners_ref[group, 1]]
         out_ref[group, :, 128:256] = jnp.concatenate([one[:, DH:], two[:, DH:]], axis=1)
-
-
-def sum_kernel(partners_ref, in_ref, out_ref, total):
+        sent.append(pltpu.make_async_copy(out_ref.at[group], out_hbm.at[group], sems.at[group]))
+        sent[-1].start()
+    for copy in sent:
+        copy.wait()
+
+
+def sum_kernel(partners_ref, in_ref, out_ref, total, second):
     groups, sent = in_ref.shape[:2]
     for group in range(groups):
         x = in_ref[group, :, 0:128].astype(F32)
         total[group, :sent] = x
         total[group, sent:] = from_spare(x, 0, (0, 2, 3))
+    second[...] = jnp.zeros_like(second)
     left = slots(sent + REST) < 2
     for group in range(groups):
         listed = in_ref[group, :, 128:256].astype(F32)
         rest = from_spare(in_ref[group, :, 0:128].astype(F32), 3 * REST, range(4))
         listed = jnp.concatenate([listed, rest], axis=0)
         one, two = partners_ref[group, 0], partners_ref[group, 1]
-        total[one] += jnp.where(left, 0.0, pltpu.roll(listed, DH, 1))
         total[two] += jnp.where(left, 0.0, listed)
+        second[one] += jnp.where(left, listed, 0.0)
     folded = out_ref.shape[1]
     for group in range(groups):
         for chunk in range(2):
-            x = total[group, chunk * (folded + REST) : (chunk + 1) * (folded + REST)]
+            rows = slice(chunk * (folded + REST), (chunk + 1) * (folded + REST))
+            x = total[group, rows] + pltpu.roll(second[group, rows], DH, 1)
             fill = [to_spare(x[folded:], slot) for slot in (0, 2, 3)]
             fill = jnp.concatenate(fill + [jnp.zeros((folded - 3 * REST, 128), F32)], axis=0)
             out_ref[2 * group + chunk] = jnp.where(spare(folded), fill, x[:folded]).astype(BF16)
@@ -153,7 +171,7 @@
         for j, (keys, q_side, _) in enumerate(terms):
             raw = lax.dot_general(keys[...], q_side, nt, preferred_element_type=F32)
             if j:
-                head = raw[:HIDDEN_MOST] + bias[j - 1, :, :size]
+                head = raw[:HIDDEN_MOST] + jnp.concatenate([bias[j - 1]] * (size // 128), axis=1)
                 raw = jnp.concatenate([head, raw[HIDDEN_MOST:]], axis=0)
             s_ref[j, :, :size] = raw
             top = jnp.maximum(top, jnp.max(raw, axis=0, keepdims=True))
@@ -215,7 +233,7 @@
             pltpu.VMEM((seq, 256), BF16),
             pltpu.VMEM((seq, 256), BF16),
             pltpu.VMEM((3, DH, seq), BF16),
-            pltpu.VMEM((2, HIDDEN_MOST, WIDE), F32),
+            pltpu.VMEM((2, HIDDEN_MOST, 128), F32),
             pltpu.VMEM((3, seq, WIDE), F32),
             pltpu.VMEM((3, seq, WIDE), F32),
             pltpu.VMEM((3, 2 * DH, seq), F32),
@@ -233,13 +251,28 @@
     pieces = 2 * width // DH
     small = pltpu.CompilerParams(vmem_limit_bytes=32 * 2**20)
     packed = pl.pallas_call(
-        pack_kernel, out_shape=shape(pieces, rows, 128), in_specs=[HBM] * 4, out_specs=VMEM, name="pack",
+        pack_kernel,
+        out_shape=shape(pieces, rows, 128),
+        in_specs=[HBM] * 4,
+        out_specs=HBM,
+        scratch_shapes=[pltpu.VMEM((rows, width), BF16)] * 4
+        + [
+            pltpu.VMEM((pieces, rows, 128), BF16),
+            pltpu.SemaphoreType.DMA((pieces // 8, 4)),
+            pltpu.SemaphoreType.DMA((pieces // 8,)),
+        ],
+        name="pack",
         compiler_params=pltpu.CompilerParams(vmem_limit_bytes=63_400_000),
-        scratch_shapes=[pltpu.VMEM((rows, width), BF16)] * 4 + [pltpu.SemaphoreType.DMA((4,))],
     )(queries[0], grad_out[0], keys_in[0], values_in[0])
     by_group = lax.all_to_all(packed, OUTER, 0, 0, tiled=True).reshape(groups, 2 * rows, 128)
     picked = pl.pallas_call(
-        pick_kernel, out_shape=shape(groups, 2 * rows, 256), in_specs=[SMEM, VMEM], out_specs=VMEM, name="pick", compiler_params=small
+        pick_kernel,
+        out_shape=shape(groups, 2 * rows, 256),
+        in_specs=[SMEM, VMEM],
+        out_specs=HBM,
+        scratch_shapes=[pltpu.VMEM((groups, 2 * rows, 256), BF16), pltpu.SemaphoreType.DMA((groups,))],
+        name="pick",
+        compiler_params=small,
     )(partners, by_group)
     gathered = lax.all_to_all(picked, INNER, 0, 0, tiled=True)
     hidden = registers[partners[lax.axis_index(INNER)]]
@@ -249,7 +282,7 @@
         out_shape=shape(pieces, rows - REST, 128),
         in_specs=[SMEM, VMEM],
         out_specs=VMEM,
-        scratch_shapes=[pltpu.VMEM((groups, 2 * rows, 128), F32)],
+        scratch_shapes=[pltpu.VMEM((groups, 2 * rows, 128), F32)] * 2,
         name="sum",
         compiler_params=small,
     )(partners, spread)

time: 121 us -> 122 us (level)
  no operation moved by 1% of the time
where the time goes in v6:
time: 122 us; the launch traced here: 120 us
  blocking collectives  43.4 us (36%)
  waiting for transfers between devices  31.9 us (26%)
  Pallas kernels  24.6 us (20%)
  starting transfers between devices  18.5 us (15%)
    all_to_all x1, blocking collectives, local(): by_head = lax.all_to_all(summed, OUTER, 0, 0, tiled=True)  28 us
    all_to_all x1, waiting for transfers between devices, local(): lax.all_to_all(packed, OUTER, 0, 0, tiled=True)  17.8 us
    pallas_call x1, Pallas kernels, attend(): pl.pallas_call(attend_kernel, out_shape=shape(rows.shape[0], rows.shape[1...  15.7 us
    all_to_all x1, blocking collectives, local(): spread = lax.all_to_all(attend(hidden, gathered), INNER, 0, 0, tiled=True)  15.4 us
    all_to_all x1, waiting for transfers between devices, local(): gathered = lax.all_to_all(picked, INNER, 0, 0, tiled=True)  14 us
    all_to_all x1, starting transfers between devices, local(): lax.all_to_all(packed, OUTER, 0, 0, tiled=True)  12.6 us
    all_to_all x1, starting transfers between devices, local(): gathered = lax.all_to_all(picked, INNER, 0, 0, tiled=True)  5.88 us
    pallas_call x1, Pallas kernels, local(): pl.pallas_call(sum_kernel, out_shape=shape(pieces, rows - REST, 128), in_...  2.85 us
  transfers between devices with their start and end apart: 2, of which 2 were waited for; matrix products, arithmetic and copies ran while one was open for 1% of the time, Pallas kernels for 0%

profile of v6, /device:TPU:1, one launch (start us, length us, event | category | flops | bytes accessed | tf_op | source)
XLA Modules:
  0.0 120.0 jit_solution(1811195403613008170)
XLA Ops:
  0.6 0.0 copy-start
  0.6 0.0 copy-start.1
  0.7 2.5 %pack.1 = bf16[32,72,128]{2,1,0:T(8,128)(2,1)} custom-call(bf16[72,1024]{1,0:T(8,128)(2,1)} %bitcast.13, bf16[72,1024]{1,0:T(8,128)(2,1)} %bitcast.14, bf16[72,1024]{1,0:T(8,128)(2,1)} %bitcast.15, bf16[72,1024]{1,0:T(8,128)(2,1)} %bitcast.16), custom_call_target="tpu_custom_call" | custom-call | tf_op jit(solution)/shard_map/pack/pallas_call | solution.py:253
  3.1 12.6 %all-to-all-start = ((bf16[32,72,128]{2,1,0:T(8,128)(2,1)}), bf16[32,72,128]{2,1,0:T(8,128)(2,1)S(1)}, u32[]{:S(2)}, u32[]{:S(2)}) async-start(bf16[32,72,128]{2,1,0:T(8,128)(2,1)} %pack.1), calls=%async_computation | async-start | bytes 1179648 | tf_op jit(solution)/shard_map/all_to_all | solution.py:267
  15.8 0.0 copy-done.1
  15.8 0.1 copy.12.partners_ref
  15.8 17.8 %all-to-all-done = bf16[32,72,128]{2,1,0:T(8,128)(2,1)S(1)} async-done(((bf16[32,72,128]{2,1,0:T(8,128)(2,1)}), bf16[32,72,128]{2,1,0:T(8,128)(2,1)S(1)}, u32[]{:S(2)}, u32[]{:S(2)}) %all-to-all-start) | async-done | bytes 589856 | tf_op jit(solution)/shard_map/all_to_all | solution.py:267
  33.7 1.9 %pick.1 = bf16[16,144,256]{2,1,0:T(8,128)(2,1)} custom-call(s32[16,2]{1,0:T(8,128)S(1)} %copy.12.partners_ref, bf16[16,144,128]{2,1,0:T(8,128)(2,1)S(1)} %bitcast.12), custom_call_target="tpu_custom_call" | custom-call | tf_op jit(solution)/shard_map/pick/pallas_call | solution.py:268
  35.6 5.9 %all-to-all-start.1 = ((bf16[16,144,256]{2,1,0:T(8,128)(2,1)}), bf16[16,144,256]{2,1,0:T(8,128)(2,1)S(1)}, u32[]{:S(2)}, u32[]{:S(2)}) async-start(bf16[16,144,256]{2,1,0:T(8,128)(2,1)} %pick.1), calls=%async_computation.1 | async-start | bytes 2359296 | tf_op jit(solution)/shard_map/all_to_all | solution.py:277
  41.5 0.2 dynamic-slice_reduce_fusion
  41.7 0.0 copy-done
  41.7 0.6 gather_fusion
  42.3 14.0 %all-to-all-done.1.in_ref = bf16[16,144,256]{2,1,0:T(8,128)(2,1)S(1)} async-done(((bf16[16,144,256]{2,1,0:T(8,128)(2,1)}), bf16[16,144,256]{2,1,0:T(8,128)(2,1)S(1)}, u32[]{:S(2)}, u32[]{:S(2)}) %all-to-all-start.1) | async-done | bytes 1179680 | tf_op jit(solution)/shard_map/all_to_all | solution.py:277
  56.4 15.7 %attend.1 = bf16[16,128,256]{2,1,0:T(8,128)(2,1)S(1)} custom-call(s32[2]{0:T(128)S(1)} %gather_fusion, bf16[16,144,256]{2,1,0:T(8,128)(2,1)S(1)} %all-to-all-done.1.in_ref), custom_call_target="tpu_custom_call" | custom-call | tf_op jit(solution)/shard_map/attend/pallas_call | solution.py:227
  72.1 15.4 %all_to_all.20.in_ref = bf16[16,128,256]{2,1,0:T(8,128)(2,1)S(1)} all-to-all(bf16[16,128,256]{2,1,0:T(8,128)(2,1)S(1)} %attend.1), channel_id=1, replica_groups=mesh['zh'=2,'x1'=2,'x0'=2,'c'=2,'y'=4,'zl1'=2,'zl0'=2] {'y','x0','zl0'}, dimensions={0} | all-to-all | bytes 2097152 | tf_op jit(solution)/shard_map/all_to_all | solution.py:279
  87.5 2.8 %sum.1 = bf16[32,56,128]{2,1,0:T(8,128)(2,1)S(1)} custom-call(s32[16,2]{1,0:T(8,128)S(1)} %copy.12.partners_ref, bf16[16,128,256]{2,1,0:T(8,128)(2,1)S(1)} %all_to_all.20.in_ref), custom_call_target="tpu_custom_call" | custom-call | tf_op jit(solution)/shard_map/sum/pallas_call | solution.py:280
  90.3 28.0 %all_to_all.21.in_ref = bf16[32,56,128]{2,1,0:T(8,128)(2,1)S(1)} all-to-all(bf16[32,56,128]{2,1,0:T(8,128)(2,1)S(1)} %sum.1), channel_id=1, replica_groups=mesh['zh'=2,'x1'=2,'x0'=2,'c'=2,'y'=4,'zl1'=2,'zl0'=2] {'zh','x1','x0','..., dimensions={0} | all-to-all | bytes 917504 | tf_op jit(solution)/shard_map/all_to_all | solution.py:289
  118.4 1.6 %unpack.1 = (bf16[72,1024]{1,0:T(8,128)(2,1)}, bf16[72,1024]{1,0:T(8,128)(2,1)}, bf16[72,1024]{1,0:T(8,128)(2,1)}) custom-call(bf16[32,56,128]{2,1,0:T(8,128)(2,1)S(1)} %all_to_all.21.in_ref), custom_call_target="tpu_custom_call" | custom-call | tf_op jit(solution)/shard_map/unpack/pallas_call | solution.py:290
  (2 shorter events, 0.0 us)
Async XLA Ops:
  0.6 41.1 %copy-start = (s32[16]{0:T(128)S(1)}, s32[16]{0:T(128)}, u32[]{:S(2)}) copy-start(s32[16]{0:T(128)} %param.11) | copy-start | bytes 196
  0.6 15.1 %copy-start.1 = (s32[16,2]{0,1:T(2,128)S(1)}, s32[16,2]{0,1:T(2,128)}, u32[]{:S(2)}) copy-start(s32[16,2]{0,1:T(2,128)} %param.10) | copy-start | bytes 388
  3.1 30.5 %all-to-all-start = ((bf16[32,72,128]{2,1,0:T(8,128)(2,1)}), bf16[32,72,128]{2,1,0:T(8,128)(2,1)S(1)}, u32[]{:S(2)}, u32[]{:S(2)}) async-start(bf16[32,72,128]{2,1,0:T(8,128)(2,1)} %pack.1), calls=%async_computation | async-start | bytes 1179648 | tf_op jit(solution)/shard_map/all_to_all | solution.py:267
  35.6 20.8 %all-to-all-start.1 = ((bf16[16,144,256]{2,1,0:T(8,128)(2,1)}), bf16[16,144,256]{2,1,0:T(8,128)(2,1)S(1)}, u32[]{:S(2)}, u32[]{:S(2)}) async-start(bf16[16,144,256]{2,1,0:T(8,128)(2,1)} %pick.1), calls=%async_computation.1 | async-start | bytes 2359296 | tf_op jit(solution)/shard_map/all_to_all | solution.py:277

commit v7 on v5

--- a/solution.py
+++ b/solution.py
@@ -18,12 +18,12 @@
 SMEM = pl.BlockSpec(memory_space=pltpu.SMEM)
 
 FINE = (("zh", 2), ("x1", 2), ("x0", 2), ("c", 2), ("y", 4), ("zl1", 2), ("zl0", 2))
-OUTER = ("zh", "x1", "x0", "c", "zl1")
-INNER = ("y", "x0", "zl0")
+OUTER = ("zl1", "zh", "x1", "x0", "c")
+INNER = ("x0", "y", "zl0")
 
 
 def piece(head, half):
-    return head // 4 * 8 + half * 4 + head % 4
+    return head // 2 * 4 + half * 2 + head % 2
 
 
 def columns(head, half):
@@ -83,10 +83,13 @@
 
 
 def pick_kernel(partners_ref, in_ref, out_ref):
-    for group in range(in_ref.shape[0]):
-        out_ref[group, :, 0:128] = in_ref[group]
-        one, two = in_ref[partners_ref[group, 0]], in_ref[partners_ref[group, 1]]
-        out_ref[group, :, 128:256] = jnp.concatenate([one[:, DH:], two[:, DH:]], axis=1)
+    groups, chunks = out_ref.shape[:2]
+    for group in range(groups):
+        for chunk in range(chunks):
+            first = chunk * groups
+            out_ref[group, chunk, :, 0:128] = in_ref[first + group]
+            one, two = (in_ref[first + partners_ref[group, slot]] for slot in range(2))
+            out_ref[group, chunk, :, 128:256] = jnp.concatenate([one[:, DH:], two[:, DH:]], axis=1)
 
 
 def sum_kernel(partners_ref, in_ref, out_ref, total):
@@ -109,7 +112,7 @@
             x = total[group, chunk * (folded + REST) : (chunk + 1) * (folded + REST)]
             fill = [to_spare(x[folded:], slot) for slot in (0, 2, 3)]
             fill = jnp.concatenate(fill + [jnp.zeros((folded - 3 * REST, 128), F32)], axis=0)
-            out_ref[2 * group + chunk] = jnp.where(spare(folded), fill, x[:folded]).astype(BF16)
+            out_ref[chunk * groups + group] = jnp.where(spare(folded), fill, x[:folded]).astype(BF16)
 
 
 WIDE = 1152
@@ -118,7 +121,7 @@
 def attend_kernel(hidden_ref, in_ref, out_ref, own, listed, kt, bias, s_ref, dp_ref, total, flat, dqt):
     sources, rows_of = in_ref.shape[:2]
     seq = own.shape[0]
-    blocks = [(s // 4 * 2 + s % 2, s // 2 % 2) for s in range(sources)]
+    blocks = [(s % (sources // 2), s // (sources // 2)) for s in range(sources)]
     for source, (block, half) in enumerate(blocks):
         rows = slice(block * rows_of, (block + 1) * rows_of)
         lanes = slice(128 * half, 128 * (half + 1))
@@ -237,11 +240,11 @@
         compiler_params=pltpu.CompilerParams(vmem_limit_bytes=63_400_000),
         scratch_shapes=[pltpu.VMEM((rows, width), BF16)] * 4 + [pltpu.SemaphoreType.DMA((4,))],
     )(queries[0], grad_out[0], keys_in[0], values_in[0])
-    by_group = lax.all_to_all(packed, OUTER, 0, 0, tiled=True).reshape(groups, 2 * rows, 128)
+    by_group = lax.all_to_all(packed, OUTER, 0, 0, tiled=True)
     picked = pl.pallas_call(
-        pick_kernel, out_shape=shape(groups, 2 * rows, 256), in_specs=[SMEM, VMEM], out_specs=VMEM, name="pick", compiler_params=small
+        pick_kernel, out_shape=shape(groups, 2, rows, 256), in_specs=[SMEM, VMEM], out_specs=VMEM, name="pick", compiler_params=small
     )(partners, by_group)
-    gathered = lax.all_to_all(picked, INNER, 0, 0, tiled=True)
+    gathered = lax.all_to_all(picked.reshape(groups, 2 * rows, 256), INNER, 0, 0, tiled=True)
     hidden = registers[partners[lax.axis_index(INNER)]]
     spread = lax.all_to_all(attend(hidden, gathered), INNER, 0, 0, tiled=True)
     summed = pl.pallas_call(

time: 121 us -> 123 us (1.017); the launches traced: 119 us -> 123 us
  waiting for transfers between devices: 31.9 us -> 37.2 us
    all_to_all x1, blocking collectives: 28 us -> 22 us  [local(): by_head = lax.all_to_all(summed, OUTER, 0, 0, tiled=True)]
    all_to_all x2, waiting for transfers between devices: 31.9 us -> 37.2 us  [the longest x1 20.3 us: local(): by_group = lax.all_to_all(packed, OUTER, 0, 0, tiled=True)]
    all_to_all x1, blocking collectives: 15.4 us -> 20.2 us  [local(): spread = lax.all_to_all(attend(hidden, gathered), INNER, 0, 0, tiled=True)]
where the time goes in v7:
time: 123 us
  blocking collectives  42.2 us (34%)
  waiting for transfers between devices  37.2 us (30%)
  Pallas kernels  24 us (20%)
  starting transfers between devices  18 us (15%)
    all_to_all x1, blocking collectives, local(): by_head = lax.all_to_all(summed, OUTER, 0, 0, tiled=True)  22 us
    all_to_all x1, waiting for transfers between devices, local(): by_group = lax.all_to_all(packed, OUTER, 0, 0, tiled=True)  20.3 us
    all_to_all x1, blocking collectives, local(): spread = lax.all_to_all(attend(hidden, gathered), INNER, 0, 0, tiled=True)  20.2 us
    all_to_all x1, waiting for transfers between devices, local(): lax.all_to_all(picked.reshape(groups, 2 * rows, 256), INNER, 0, 0, tiled=...  16.9 us
    pallas_call x1, Pallas kernels, attend(): pl.pallas_call(attend_kernel, out_shape=shape(rows.shape[0], rows.shape[1...  15.7 us
    all_to_all x1, starting transfers between devices, local(): by_group = lax.all_to_all(packed, OUTER, 0, 0, tiled=True)  12.6 us
    all_to_all x1, starting transfers between devices, local(): lax.all_to_all(picked.reshape(groups, 2 * rows, 256), INNER, 0, 0, tiled=...  5.37 us
    pallas_call x1, Pallas kernels, local(): pl.pallas_call(pack_kernel, out_shape=shape(pieces, rows, 128), in_specs=...  2.57 us
  transfers between devices with their start and end apart: 2, of which 2 were waited for; matrix products, arithmetic and copies ran while one was open for 1% of the time, Pallas kernels for 0%

profile of v7, /device:TPU:1, one launch (start us, length us, event | category | flops | bytes accessed | tf_op | source)
XLA Modules:
  0.0 123.0 jit_solution(12142110691626746455)
XLA Ops:
  0.6 0.0 copy-start
  0.6 0.0 copy-start.1
  0.7 2.6 %pack.1 = bf16[32,72,128]{2,1,0:T(8,128)(2,1)} custom-call(bf16[72,1024]{1,0:T(8,128)(2,1)} %bitcast.12, bf16[72,1024]{1,0:T(8,128)(2,1)} %bitcast.13, bf16[72,1024]{1,0:T(8,128)(2,1)} %bitcast.14, bf16[72,1024]{1,0:T(8,128)(2,1)} %bitcast.15), custom_call_target="tpu_custom_call" | custom-call | tf_op jit(solution)/shard_map/pack/pallas_call | solution.py:238
  3.2 12.6 %all-to-all-start = ((bf16[32,72,128]{2,1,0:T(8,128)(2,1)}), bf16[32,72,128]{2,1,0:T(8,128)(2,1)S(1)}, u32[]{:S(2)}, u32[]{:S(2)}) async-start(bf16[32,72,128]{2,1,0:T(8,128)(2,1)} %pack.1), calls=%async_computation | async-start | bytes 1179648 | tf_op jit(solution)/shard_map/all_to_all | solution.py:243
  15.8 0.0 copy-done.1
  15.8 0.1 copy.12.partners_ref
  15.9 20.3 %all-to-all-done.in_ref = bf16[32,72,128]{2,1,0:T(8,128)(2,1)S(1)} async-done(((bf16[32,72,128]{2,1,0:T(8,128)(2,1)}), bf16[32,72,128]{2,1,0:T(8,128)(2,1)S(1)}, u32[]{:S(2)}, u32[]{:S(2)}) %all-to-all-start) | async-done | bytes 589856 | tf_op jit(solution)/shard_map/all_to_all | solution.py:243
  36.2 2.0 %pick.1 = bf16[16,2,72,256]{3,2,1,0:T(8,128)(2,1)} custom-call(s32[16,2]{1,0:T(8,128)S(1)} %copy.12.partners_ref, bf16[32,72,128]{2,1,0:T(8,128)(2,1)S(1)} %all-to-all-done.in_ref), custom_call_target="tpu_custom_call" | custom-call | tf_op jit(solution)/shard_map/pick/pallas_call | solution.py:244
  38.2 5.4 %all-to-all-start.1 = ((bf16[16,144,256]{2,1,0:T(8,128)(2,1)}), bf16[16,144,256]{2,1,0:T(8,128)(2,1)S(1)}, u32[]{:S(2)}, u32[]{:S(2)}) async-start(bf16[16,144,256]{2,1,0:T(8,128)(2,1)} %bitcast.5), calls=%async_computation.1 | async-start | bytes 2359296 | tf_op jit(solution)/shard_map/all_to_all | solution.py:247
  43.6 0.2 dynamic-slice_reduce_fusion
  43.8 0.0 copy-done
  43.8 0.6 gather_fusion
  44.4 16.9 %all-to-all-done.1.in_ref = bf16[16,144,256]{2,1,0:T(8,128)(2,1)S(1)} async-done(((bf16[16,144,256]{2,1,0:T(8,128)(2,1)}), bf16[16,144,256]{2,1,0:T(8,128)(2,1)S(1)}, u32[]{:S(2)}, u32[]{:S(2)}) %all-to-all-start.1) | async-done | bytes 1179680 | tf_op jit(solution)/shard_map/all_to_all | solution.py:247
  61.3 15.7 %attend.1 = bf16[16,128,256]{2,1,0:T(8,128)(2,1)S(1)} custom-call(s32[2]{0:T(128)S(1)} %gather_fusion, bf16[16,144,256]{2,1,0:T(8,128)(2,1)S(1)} %all-to-all-done.1.in_ref), custom_call_target="tpu_custom_call" | custom-call | tf_op jit(solution)/shard_map/attend/pallas_call | solution.py:212
  77.0 20.2 %all_to_all.20.in_ref = bf16[16,128,256]{2,1,0:T(8,128)(2,1)S(1)} all-to-all(bf16[16,128,256]{2,1,0:T(8,128)(2,1)S(1)} %attend.1), channel_id=1, replica_groups=mesh['zh'=2,'x1'=2,'x0'=2,'c'=2,'y'=4,'zl1'=2,'zl0'=2] {'x0','y','zl0'}, dimensions={0} | all-to-all | bytes 2097152 | tf_op jit(solution)/shard_map/all_to_all | solution.py:249
  97.3 2.1 %sum.1 = bf16[32,56,128]{2,1,0:T(8,128)(2,1)S(1)} custom-call(s32[16,2]{1,0:T(8,128)S(1)} %copy.12.partners_ref, bf16[16,128,256]{2,1,0:T(8,128)(2,1)S(1)} %all_to_all.20.in_ref), custom_call_target="tpu_custom_call" | custom-call | tf_op jit(solution)/shard_map/sum/pallas_call | solution.py:250
  99.4 22.0 %all_to_all.21.in_ref = bf16[32,56,128]{2,1,0:T(8,128)(2,1)S(1)} all-to-all(bf16[32,56,128]{2,1,0:T(8,128)(2,1)S(1)} %sum.1), channel_id=1, replica_groups=mesh['zh'=2,'x1'=2,'x0'=2,'c'=2,'y'=4,'zl1'=2,'zl0'=2] {'zl1','zh','x1',..., dimensions={0} | all-to-all | bytes 917504 | tf_op jit(solution)/shard_map/all_to_all | solution.py:259
  121.4 1.6 %unpack.1 = (bf16[72,1024]{1,0:T(8,128)(2,1)}, bf16[72,1024]{1,0:T(8,128)(2,1)}, bf16[72,1024]{1,0:T(8,128)(2,1)}) custom-call(bf16[32,56,128]{2,1,0:T(8,128)(2,1)S(1)} %all_to_all.21.in_ref), custom_call_target="tpu_custom_call" | custom-call | tf_op jit(solution)/shard_map/unpack/pallas_call | solution.py:260
  (2 shorter events, 0.0 us)
Async XLA Ops:
  0.6 43.2 %copy-start = (s32[16]{0:T(128)S(1)}, s32[16]{0:T(128)}, u32[]{:S(2)}) copy-start(s32[16]{0:T(128)} %param.11) | copy-start | bytes 196
  0.6 15.2 %copy-start.1 = (s32[16,2]{0,1:T(2,128)S(1)}, s32[16,2]{0,1:T(2,128)}, u32[]{:S(2)}) copy-start(s32[16,2]{0,1:T(2,128)} %param.10) | copy-start | bytes 388
  3.2 33.0 %all-to-all-start = ((bf16[32,72,128]{2,1,0:T(8,128)(2,1)}), bf16[32,72,128]{2,1,0:T(8,128)(2,1)S(1)}, u32[]{:S(2)}, u32[]{:S(2)}) async-start(bf16[32,72,128]{2,1,0:T(8,128)(2,1)} %pack.1), calls=%async_computation | async-start | bytes 1179648 | tf_op jit(solution)/shard_map/all_to_all | solution.py:243
  38.2 23.1 %all-to-all-start.1 = ((bf16[16,144,256]{2,1,0:T(8,128)(2,1)}), bf16[16,144,256]{2,1,0:T(8,128)(2,1)S(1)}, u32[]{:S(2)}, u32[]{:S(2)}) async-start(bf16[16,144,256]{2,1,0:T(8,128)(2,1)} %bitcast.5), calls=%async_computation.1 | async-start | bytes 2359296 | tf_op jit(solution)/shard_map/all_to_all | solution.py:247

commit v8 on v7

--- a/solution.py
+++ b/solution.py
@@ -19,7 +19,7 @@
 
 FINE = (("zh", 2), ("x1", 2), ("x0", 2), ("c", 2), ("y", 4), ("zl1", 2), ("zl0", 2))
 OUTER = ("zl1", "zh", "x1", "x0", "c")
-INNER = ("x0", "y", "zl0")
+INNER = ("y", "x0", "zl0")
 
 
 def piece(head, half):
@@ -121,7 +121,7 @@
 def attend_kernel(hidden_ref, in_ref, out_ref, own, listed, kt, bias, s_ref, dp_ref, total, flat, dqt):
     sources, rows_of = in_ref.shape[:2]
     seq = own.shape[0]
-    blocks = [(s % (sources // 2), s // (sources // 2)) for s in range(sources)]
+    blocks = [(s // 4 * 2 + s % 2, s // 2 % 2) for s in range(sources)]
     for source, (block, half) in enumerate(blocks):
         rows = slice(block * rows_of, (block + 1) * rows_of)
         lanes = slice(128 * half, 128 * (half + 1))

time: 123 us -> 124 us (level)
  no operation moved by 1% of the time
where the time goes in v8:
time: 124 us; the launch traced here: 123 us
  blocking collectives  43.3 us (35%)
  waiting for transfers between devices  36.4 us (29%)
  Pallas kernels  24 us (19%)
  starting transfers between devices  18 us (15%)
    all_to_all x1, blocking collectives, local(): by_head = lax.all_to_all(summed, OUTER, 0, 0, tiled=True)  23.1 us
    all_to_all x1, waiting for transfers between devices, local(): by_group = lax.all_to_all(packed, OUTER, 0, 0, tiled=True)  20.3 us
    all_to_all x1, blocking collectives, local(): spread = lax.all_to_all(attend(hidden, gathered), INNER, 0, 0, tiled=True)  20.2 us
    all_to_all x1, waiting for transfers between devices, local(): lax.all_to_all(picked.reshape(groups, 2 * rows, 256), INNER, 0, 0, tiled=...  16.1 us
    pallas_call x1, Pallas kernels, attend(): pl.pallas_call(attend_kernel, out_shape=shape(rows.shape[0], rows.shape[1...  15.7 us
    all_to_all x1, starting transfers between devices, local(): by_group = lax.all_to_all(packed, OUTER, 0, 0, tiled=True)  12.6 us
    all_to_all x1, starting transfers between devices, local(): lax.all_to_all(picked.reshape(groups, 2 * rows, 256), INNER, 0, 0, tiled=...  5.37 us
    pallas_call x1, Pallas kernels, local(): pl.pallas_call(pack_kernel, out_shape=shape(pieces, rows, 128), in_specs=...  2.57 us
  transfers between devices with their start and end apart: 2, of which 2 were waited for; matrix products, arithmetic and copies ran while one was open for 1% of the time, Pallas kernels for 0%

profile of v8, /device:TPU:1, one launch (start us, length us, event | category | flops | bytes accessed | tf_op | source)
XLA Modules:
  0.0 123.3 jit_solution(17662558029866807365)
XLA Ops:
  0.6 0.0 copy-start
  0.6 0.0 copy-start.1
  0.7 2.6 %pack.1 = bf16[32,72,128]{2,1,0:T(8,128)(2,1)} custom-call(bf16[72,1024]{1,0:T(8,128)(2,1)} %bitcast.12, bf16[72,1024]{1,0:T(8,128)(2,1)} %bitcast.13, bf16[72,1024]{1,0:T(8,128)(2,1)} %bitcast.14, bf16[72,1024]{1,0:T(8,128)(2,1)} %bitcast.15), custom_call_target="tpu_custom_call" | custom-call | tf_op jit(solution)/shard_map/pack/pallas_call | solution.py:238
  3.2 12.6 %all-to-all-start = ((bf16[32,72,128]{2,1,0:T(8,128)(2,1)}), bf16[32,72,128]{2,1,0:T(8,128)(2,1)S(1)}, u32[]{:S(2)}, u32[]{:S(2)}) async-start(bf16[32,72,128]{2,1,0:T(8,128)(2,1)} %pack.1), calls=%async_computation | async-start | bytes 1179648 | tf_op jit(solution)/shard_map/all_to_all | solution.py:243
  15.8 0.0 copy-done.1
  15.8 0.1 copy.12.partners_ref
  15.9 20.3 %all-to-all-done.in_ref = bf16[32,72,128]{2,1,0:T(8,128)(2,1)S(1)} async-done(((bf16[32,72,128]{2,1,0:T(8,128)(2,1)}), bf16[32,72,128]{2,1,0:T(8,128)(2,1)S(1)}, u32[]{:S(2)}, u32[]{:S(2)}) %all-to-all-start) | async-done | bytes 589856 | tf_op jit(solution)/shard_map/all_to_all | solution.py:243
  36.2 2.0 %pick.1 = bf16[16,2,72,256]{3,2,1,0:T(8,128)(2,1)} custom-call(s32[16,2]{1,0:T(8,128)S(1)} %copy.12.partners_ref, bf16[32,72,128]{2,1,0:T(8,128)(2,1)S(1)} %all-to-all-done.in_ref), custom_call_target="tpu_custom_call" | custom-call | tf_op jit(solution)/shard_map/pick/pallas_call | solution.py:244
  38.2 5.4 %all-to-all-start.1 = ((bf16[16,144,256]{2,1,0:T(8,128)(2,1)}), bf16[16,144,256]{2,1,0:T(8,128)(2,1)S(1)}, u32[]{:S(2)}, u32[]{:S(2)}) async-start(bf16[16,144,256]{2,1,0:T(8,128)(2,1)} %bitcast.5), calls=%async_computation.1 | async-start | bytes 2359296 | tf_op jit(solution)/shard_map/all_to_all | solution.py:247
  43.6 0.2 dynamic-slice_reduce_fusion
  43.8 0.0 copy-done
  43.8 0.6 gather_fusion
  44.4 16.1 %all-to-all-done.1.in_ref = bf16[16,144,256]{2,1,0:T(8,128)(2,1)S(1)} async-done(((bf16[16,144,256]{2,1,0:T(8,128)(2,1)}), bf16[16,144,256]{2,1,0:T(8,128)(2,1)S(1)}, u32[]{:S(2)}, u32[]{:S(2)}) %all-to-all-start.1) | async-done | bytes 1179680 | tf_op jit(solution)/shard_map/all_to_all | solution.py:247
  60.6 15.7 %attend.1 = bf16[16,128,256]{2,1,0:T(8,128)(2,1)S(1)} custom-call(s32[2]{0:T(128)S(1)} %gather_fusion, bf16[16,144,256]{2,1,0:T(8,128)(2,1)S(1)} %all-to-all-done.1.in_ref), custom_call_target="tpu_custom_call" | custom-call | tf_op jit(solution)/shard_map/attend/pallas_call | solution.py:212
  76.3 20.2 %all_to_all.20.in_ref = bf16[16,128,256]{2,1,0:T(8,128)(2,1)S(1)} all-to-all(bf16[16,128,256]{2,1,0:T(8,128)(2,1)S(1)} %attend.1), channel_id=1, replica_groups=mesh['zh'=2,'x1'=2,'x0'=2,'c'=2,'y'=4,'zl1'=2,'zl0'=2] {'y','x0','zl0'}, dimensions={0} | all-to-all | bytes 2097152 | tf_op jit(solution)/shard_map/all_to_all | solution.py:249
  96.5 2.1 %sum.1 = bf16[32,56,128]{2,1,0:T(8,128)(2,1)S(1)} custom-call(s32[16,2]{1,0:T(8,128)S(1)} %copy.12.partners_ref, bf16[16,128,256]{2,1,0:T(8,128)(2,1)S(1)} %all_to_all.20.in_ref), custom_call_target="tpu_custom_call" | custom-call | tf_op jit(solution)/shard_map/sum/pallas_call | solution.py:250
  98.6 23.1 %all_to_all.21.in_ref = bf16[32,56,128]{2,1,0:T(8,128)(2,1)S(1)} all-to-all(bf16[32,56,128]{2,1,0:T(8,128)(2,1)S(1)} %sum.1), channel_id=1, replica_groups=mesh['zh'=2,'x1'=2,'x0'=2,'c'=2,'y'=4,'zl1'=2,'zl0'=2] {'zl1','zh','x1',..., dimensions={0} | all-to-all | bytes 917504 | tf_op jit(solution)/shard_map/all_to_all | solution.py:259
  121.7 1.6 %unpack.1 = (bf16[72,1024]{1,0:T(8,128)(2,1)}, bf16[72,1024]{1,0:T(8,128)(2,1)}, bf16[72,1024]{1,0:T(8,128)(2,1)}) custom-call(bf16[32,56,128]{2,1,0:T(8,128)(2,1)S(1)} %all_to_all.21.in_ref), custom_call_target="tpu_custom_call" | custom-call | tf_op jit(solution)/shard_map/unpack/pallas_call | solution.py:260
  (2 shorter events, 0.0 us)
Async XLA Ops:
  0.6 43.2 %copy-start = (s32[16]{0:T(128)S(1)}, s32[16]{0:T(128)}, u32[]{:S(2)}) copy-start(s32[16]{0:T(128)} %param.11) | copy-start | bytes 196
  0.6 15.2 %copy-start.1 = (s32[16,2]{0,1:T(2,128)S(1)}, s32[16,2]{0,1:T(2,128)}, u32[]{:S(2)}) copy-start(s32[16,2]{0,1:T(2,128)} %param.10) | copy-start | bytes 388
  3.2 33.0 %all-to-all-start = ((bf16[32,72,128]{2,1,0:T(8,128)(2,1)}), bf16[32,72,128]{2,1,0:T(8,128)(2,1)S(1)}, u32[]{:S(2)}, u32[]{:S(2)}) async-start(bf16[32,72,128]{2,1,0:T(8,128)(2,1)} %pack.1), calls=%async_computation | async-start | bytes 1179648 | tf_op jit(solution)/shard_map/all_to_all | solution.py:243
  38.2 22.3 %all-to-all-start.1 = ((bf16[16,144,256]{2,1,0:T(8,128)(2,1)}), bf16[16,144,256]{2,1,0:T(8,128)(2,1)S(1)}, u32[]{:S(2)}, u32[]{:S(2)}) async-start(bf16[16,144,256]{2,1,0:T(8,128)(2,1)} %bitcast.5), calls=%async_computation.1 | async-start | bytes 2359296 | tf_op jit(solution)/shard_map/all_to_all | solution.py:247
